TPU v7x, 768 devices: a whole 4x8x12 slice. The times are simulated.
768 devices in a mesh: row: 48 (over x, z_lo, core), col: 16 (over y, z_hi).
Axes of the slice: x: 4, y: 8, z: 12 (z_hi: 2, z_lo: 6; z = z_hi * 6 + z_lo), core: 2. Of those that a mesh axis runs over, the one named last changes fastest.
Arguments:
- samples: bfloat16 [384, 36864], P('col', 'row'), may hold values from -6 to 6
- cotangent: bfloat16 [384, 24576], P('row', 'col'), may hold values from -12 to 12
- weight: bfloat16 [36864, 24576], P('row', 'col'), may hold values from -0.03125 to 0.03125
- row_second: float32 [36864], P('row'), may hold values from 0.5 to 30
- col_second: float32 [24576], P('col'), may hold values from 1 to 10
Outputs:
- input_grad: bfloat16 [384, 36864], P('col', 'row')
- new_weight: bfloat16 [36864, 24576], P('row', 'col')
- new_row: float32 [36864], P('row')
- new_col: float32 [24576], P('col')
All inputs are finite; a program needn't handle non-finite values.
Results may differ from a plain program's by a relative error of at most 0.0029.
The roundings to bfloat16 on the way count: a program that leaves them out, or rounds other values in their place, can miss the bound.
Values may be sent and summed in bfloat16 or wider, within the bound.
No kernel may reach another device: no remote copies, remote signals or barrier semaphores. Data moves between devices by JAX's collectives and lax.ppermute only.
A program may use at most 32 MiB of HBM per device.

v0:
```python
import jax
import jax.numpy as jnp
from jax import lax
from jax.sharding import PartitionSpec as P

WIN = 36864
WOUT = 24576
ADAM_STEP = 10


def silu_slope(preact):
    sig = jax.nn.sigmoid(preact)
    return sig * (1.0 + preact * (1.0 - sig))


def local(samples, cotangent, weight, row_second, col_second):
    gathered = lax.all_gather(samples, "col", axis=0, tiled=True)
    partial_sum = jnp.dot(gathered, weight, preferred_element_type=jnp.float32)
    preact_all = lax.psum(partial_sum, "row")
    cot_all = lax.all_gather(cotangent, "row", axis=0, tiled=True)
    slope_all = (cot_all.astype(jnp.float32) * silu_slope(preact_all)).astype(jnp.bfloat16)
    input_grad = lax.psum_scatter(
        lax.dot_general(
            slope_all, weight, (((1,), (1,)), ((), ())), preferred_element_type=jnp.float32
        ),
        "col",
        scatter_dimension=0,
        tiled=True,
    ).astype(jnp.bfloat16)
    grad = lax.dot_general(
        gathered, slope_all, (((0,), (0,)), ((), ())), preferred_element_type=jnp.float32
    )
    squared = grad * grad
    row_total = lax.psum(jnp.sum(squared, axis=1), "col")
    new_row = 0.999 * row_second + 0.001 * (row_total / WOUT)
    col_total, row_factor_sum = lax.psum((jnp.sum(squared, axis=0), jnp.sum(new_row)), "row")
    new_col = 0.999 * col_second + 0.001 * (col_total / WIN)
    scale = row_factor_sum / WIN
    fix_two = 1.0 - 0.999**ADAM_STEP
    second = new_row[:, None] * new_col[None, :] / scale
    update = grad / (jnp.sqrt(second / fix_two) + 1e-08)
    new_weight = (weight.astype(jnp.float32) - 0.01 * update).astype(jnp.bfloat16)
    return (input_grad, new_weight, new_row, new_col)


def solution(mesh):
    in_specs = (P("col", "row"), P("row", "col"), P("row", "col"), P("row"), P("col"))
    out_specs = (P("col", "row"), P("row", "col"), P("row"), P("col"))
    return jax.shard_map(local, mesh=mesh, in_specs=in_specs, out_specs=out_specs, check_vma=False)
```

profile of v0, /device:TPU:1, one launch (start us, length us, event | category | flops | bytes accessed | tf_op | source)
XLA Modules:
  0.0 945.3 jit_solution(4968321316379524267)
XLA Ops:
  7.2 0.0 all-gather.2.cloned.1.call-start
  7.2 0.7 all-gather.2.cloned.1.call-update
  7.9 0.0 all-reduce.3.cloned.1.call-start
  7.9 88.0 %all_gather.7 = bf16[384,768]{1,0:T(8,128)(2,1)S(1)} all-gather(bf16[24,768]{1,0:T(8,128)(2,1)} %param.5), channel_id=1, replica_groups=mesh['row'=48,'col'=16] {'col'}, dimensions={0}, use_global_device_ids=true | all-gather | bytes 626688 | tf_op jit(solution)/shard_map/all_gather | solution.py:17
  96.0 0.0 copy-start.1
  96.0 0.8 copy-done.1
  96.8 4.1 fusion.6
  101.0 0.0 all-reduce.3.cloned.1.call-update
  101.0 0.0 reduce-scatter.2.cloned.1.call-start
  101.0 2.8 copy.9
  103.9 17.5 %all-gather.2.cloned.1.call-done = bf16[384,1536]{1,0:T(8,128)(2,1)} async-done(((bf16[8,1536]{1,0:T(8,128)(2,1)}), bf16[384,1536]{1,0:T(8,128)(2,1)}) %all-gather.2.cloned.1.call-update) | async-done | bytes 1179664 | tf_op jit(solution)/shard_map/all_gather | solution.py:20
  121.4 569.3 %all-reduce.3.cloned.1.call-done = f32[384,1536]{1,0:T(8,128)} async-done(((f32[384,1536]{1,0:T(8,128)}), f32[384,1536]{1,0:T(8,128)}) %all-reduce.3.cloned.1.call-update) | async-done | bytes 2359312 | tf_op jit(solution)/shard_map/psum | solution.py:19
  690.7 0.0 copy-start
  690.7 3.1 multiply_convert_fusion
  693.8 0.0 copy-done
  693.8 2.1 fusion.7
  695.9 0.0 reduce-scatter.2.cloned.1.call-update
  695.9 0.0 copy-start.4
  695.9 5.2 fusion.3
  701.2 55.2 %psum.29 = f32[768]{0:T(1024)S(1)} all-reduce(f32[768]{0:T(1024)} %get-tuple-element.9), channel_id=1, replica_groups=mesh['row'=48,'col'=16] {'col'}, use_global_device_ids=true, to_apply=%region_3.0 | all-reduce | flops 768 | bytes 6144 | tf_op jit(solution)/shard_map/psum | solution.py:34
  756.4 1.3 fusion.5
  757.7 0.0 copy-start.3
  757.7 152.6 %all-reduce = (f32[]{:T(128)}, f32[1536]{0:T(1024)S(1)}) all-reduce(f32[]{:T(128)} %get-tuple-element.12, f32[1536]{0:T(1024)S(1)} %get-tuple-element.8), channel_id=1, replica_groups=mesh['row'=48,'col'=16] {'row'}, use_global_device_ids=true, to_apply=%region_7.0 | all-reduce | flops 1537 | bytes 12296 | tf_op jit(solution)/shard_map/psum | solution.py:36
  911.0 0.0 copy-done.4
  911.0 0.0 copy-start.2
  911.0 5.5 fusion.2
  916.5 0.0 copy-done.3
  916.5 0.0 copy-done.2
  916.5 4.3 copy.10
  920.8 16.5 %reduce-scatter.2.cloned.1.call-done = f32[24,768]{1,0:T(8,128)} async-done(((f32[384,768]{1,0:T(8,128)}), f32[24,768]{1,0:T(8,128)}) %reduce-scatter.2.cloned.1.call-update) | async-done | bytes 73744 | tf_op jit(solution)/shard_map/reduce_scatter | solution.py:22
  937.3 1.5 convert_element_type.17
  (1 shorter events, 0.0 us)
Async XLA Ops:
  7.2 114.3 %all-gather.2.cloned.1.call-start = ((), (), s32[]{:S(2)}) async-start(), calls=%async_computation.1 | async-start | bytes 1204224 | tf_op jit(solution)/shard_map/all_gather | solution.py:20
  7.9 682.8 %all-reduce.3.cloned.1.call-start = ((), (), s32[]{:S(2)}) async-start(), calls=%async_computation.2 | async-start | bytes 4718592 | tf_op jit(solution)/shard_map/psum | solution.py:19
  96.0 0.8 copy-start.1
  101.0 836.3 %reduce-scatter.2.cloned.1.call-start = ((), (), s32[]{:S(2)}) async-start(), calls=%async_computation.3 | async-start | bytes 1253376 | tf_op jit(solution)/shard_map/reduce_scatter | solution.py:22
  690.7 3.1 copy-start
  695.9 215.0 %copy-start.4 = (f32[1536]{0:T(1024)S(1)}, f32[1536]{0:T(1024)}, u32[]{:S(2)}) copy-start(f32[1536]{0:T(1024)} %param.9) | copy-start | bytes 18436
  757.7 158.8 %copy-start.3 = (f32[768]{0:T(1024)}, f32[768]{0:T(1024)S(1)}, u32[]{:S(2)}) copy-start(f32[768]{0:T(1024)S(1)} %get-tuple-element.13) | copy-start | bytes 9220
  911.0 5.5 copy-start.2
Sparse Core Ops, SparseCore 0:
  10.5 110.8 all-gather.1
  125.2 565.4 all-reduce.2
  696.6 240.6 reduce-scatter.1
where the time goes:
time: 949 us; the launch traced here: 945 us
  waiting for transfers between devices  604 us (64%)
  blocking collectives  296 us (31%)
  between operations  14.5 us (2%)
  matrix products  11.5 us (1%)
  other arithmetic  11.4 us (1%)
    psum x1, waiting for transfers between devices, local(): preact_all = lax.psum(partial_sum, 'row')  569 us
    psum x1, blocking collectives, local(): lax.psum((jnp.sum(squared, axis=0), jnp.sum(new_row)), 'row')  153 us
    all_gather x1, blocking collectives, local(): gathered = lax.all_gather(samples, 'col', axis=0, tiled=True)  88 us
    psum x1, blocking collectives, local(): row_total = lax.psum(jnp.sum(squared, axis=1), 'col')  55.2 us
  transfers between devices with their start and end apart: 3, of which 3 were waited for; matrix products, arithmetic and copies ran while one was open for 2% of the time, Pallas kernels for 0%

commit v1 on v0

v1 whole, which is shorter than its diff:
```python
import jax
import jax.numpy as jnp
from jax import lax
from jax.sharding import Mesh
from jax.sharding import PartitionSpec as P

WIN = 36864
WOUT = 24576
ADAM_STEP = 10
WEIGHT_MAX = 0.03125
GRAM_SCALE = 1.0 / 32.0

X, ZL, CORE, Y, ZH = 4, 6, 2, 8, 2
ROWS = X * ZL * CORE
COLS = Y * ZH
f32, f16, bf16 = jnp.float32, jnp.float16, jnp.bfloat16


def silu_slope(preact):
    sig = jax.nn.sigmoid(preact)
    return sig * (1.0 + preact * (1.0 - sig))


def exchange(blocks, axis):
    return lax.all_to_all(blocks, axis, 0, 0)


def gather(block, axis, size):
    return exchange(jnp.broadcast_to(block[None], (size,) + block.shape), axis)


def exponent(bound):
    return jnp.ceil(jnp.log2(jnp.maximum(bound, 1e-30))) - 15.0


def split(value, kind):
    info = jnp.finfo(kind)
    high = lax.reduce_precision(value, info.nexp, info.nmant)
    return high.astype(kind), value - high


def split16(value):
    high, rest = split(value, f16)
    return high, (rest * 2048.0).astype(f16)


def local(samples, cotangent, weight, row_second, col_second):
    own, win = samples.shape
    share, wout = cotangent.shape
    batch = own * COLS

    gathered = gather(samples, ("y", "zh"), COLS).reshape(X, ZL, CORE, share, win)
    gathered = gathered.transpose(2, 0, 1, 3, 4).reshape(batch, win)

    partial = jnp.dot(gathered, weight, preferred_element_type=f32)
    gram = lax.dot_general(gathered, gathered, (((1,), (1,)), ((), ())), preferred_element_type=f32)
    sums = jnp.concatenate([partial, gram * GRAM_SCALE], axis=1)
    for axis, size in (("core", CORE), ("x", X), ("zl", ZL)):
        blocks = sums.astype(f16).reshape(size, sums.shape[0] // size, sums.shape[1])
        sums = jnp.sum(exchange(blocks, axis).astype(f32), axis=0)
    slope = (cotangent.astype(f32) * silu_slope(sums[:, :wout])).astype(bf16)

    gram_high, gram_low = split(sums[:, wout:], bf16)
    second_one, rest = split(jnp.sum(row_second), bf16)
    second_two, second_three = split(rest, bf16)
    lanes = lax.broadcasted_iota(jnp.int32, (share, 128), 1)
    seconds = jnp.where(lanes == 0, second_one, jnp.where(lanes == 1, second_two, second_three.astype(bf16)))
    packed = jnp.concatenate([slope, gram_high, gram_low.astype(bf16), seconds], axis=1)
    for axis, size in (("zl", ZL), ("x", X), ("core", CORE)):
        packed = gather(packed, axis, size).reshape(packed.shape[0] * size, packed.shape[1])
    slope = packed[:, :wout]
    gram_high = packed[:, wout : wout + batch]
    gram_low = packed[:, wout + batch : wout + 2 * batch]
    seconds = packed.reshape(ROWS, share, -1)[:, 0, wout + 2 * batch :].astype(f32)
    second_total = jnp.sum(seconds[:, :3])

    mixed = jnp.dot(gram_high, slope, preferred_element_type=f32) + jnp.dot(gram_low, slope, preferred_element_type=f32)
    col_total = jnp.sum(slope.astype(f32) * mixed, axis=0) / GRAM_SCALE
    new_col = 0.999 * col_second + 0.001 * (col_total / WIN)
    all_total = jnp.sum(col_total)

    grad = lax.dot_general(gathered, slope, (((0,), (0,)), ((), ())), preferred_element_type=f32)
    row_total = jnp.sum(grad * grad, axis=1)

    partial = lax.dot_general(slope, weight, (((1,), (1,)), ((), ())), preferred_element_type=f32)
    partial = partial.reshape(CORE, X, ZL, share, win).transpose(1, 2, 0, 3, 4).reshape(COLS, own, win)
    grad_exp = exponent(jnp.max(jnp.abs(slope)).astype(f32) * (WEIGHT_MAX * wout))
    row_exp = exponent(jnp.max(row_total))
    total_exp = exponent(all_total)
    row_high, row_low = split16(row_total * jnp.exp2(-row_exp))
    total_high, total_low = split16(all_total * jnp.exp2(-total_exp))
    scalars = jnp.zeros((128,), f16)
    for i, value in enumerate((grad_exp, row_exp, total_exp, total_high, total_low)):
        scalars = jnp.where(lax.broadcasted_iota(jnp.int32, (128,), 0) == i, value.astype(f16), scalars)
    groups = win // 128
    side = jnp.concatenate(
        [row_high.reshape(groups, 128), row_low.reshape(groups, 128), scalars[None],
         jnp.zeros((own - 2 * groups - 1, 128), f16)], axis=0
    )
    message = jnp.concatenate(
        [(partial * jnp.exp2(-grad_exp)).astype(f16), jnp.broadcast_to(side[None], (COLS, own, 128))], axis=2
    )
    message = exchange(message, ("y", "zh")).astype(f32)
    scalars = message[:, 2 * groups, win:]
    input_grad = jnp.sum(message[:, :, :win] * jnp.exp2(scalars[:, 0])[:, None, None], axis=0).astype(bf16)
    row_parts = message[:, :groups, win:] + message[:, groups : 2 * groups, win:] * (1.0 / 2048.0)
    row_total = jnp.sum(row_parts * jnp.exp2(scalars[:, 1])[:, None, None], axis=0).reshape(win)
    all_total = jnp.sum((scalars[:, 3] + scalars[:, 4] * (1.0 / 2048.0)) * jnp.exp2(scalars[:, 2]))

    new_row = 0.999 * row_second + 0.001 * (row_total / WOUT)
    scale = 0.999 * (second_total / WIN) + 0.001 * (all_total / WOUT / WIN)
    fix_two = 1.0 - 0.999**ADAM_STEP
    row_root = jnp.sqrt(new_row / (scale * fix_two))
    col_root = jnp.sqrt(new_col)
    update = grad / (row_root[:, None] * col_root[None, :] + 1e-08)
    new_weight = (weight.astype(f32) - 0.01 * update).astype(bf16)
    return (input_grad, new_weight, new_row, new_col)


def solution(mesh):
    fine = Mesh(mesh.devices.reshape(X, ZL, CORE, Y, ZH), ("x", "zl", "core", "y", "zh"))
    row, col = ("x", "zl", "core"), ("y", "zh")
    in_specs = (P(col, row), P(row, col), P(row, col), P(row), P(col))
    out_specs = (P(col, row), P(row, col), P(row), P(col))
    return jax.shard_map(local, mesh=fine, in_specs=in_specs, out_specs=out_specs, check_vma=False)
```

time: 949 us -> 203 us (0.21)
  the two profiles are of different devices: /device:TPU:1 before, /device:TPU:264 now
where the time goes in v1:
time: 203 us; the launch traced here: 202 us
  blocking collectives  90.7 us (45%)
  waiting for transfers between devices  49.1 us (24%)
  starting transfers between devices  16.7 us (8%)
  other arithmetic  12.9 us (6%)
  between operations  11.9 us (6%)
  local copies, waits for them, and re-layouts  10.8 us (5%)
  matrix products  9.48 us (5%)
    all_to_all x5, blocking collectives, exchange(): return lax.all_to_all(blocks, axis, 0, 0)  90.7 us
    all_to_all x3, waiting for transfers between devices, exchange(): return lax.all_to_all(blocks, axis, 0, 0)  49.1 us
    all_to_all x3, starting transfers between devices, exchange(): return lax.all_to_all(blocks, axis, 0, 0)  16.7 us
    unnamed x13, local copies, waits for them, and re-layouts  8.57 us
    convert_element_type x1, other arithmetic, local(): new_weight = (weight.astype(f32) - 0.01 * update).astype(bf16)  4.15 us
  transfers between devices with their start and end apart: 3, of which 3 were waited for; matrix products, arithmetic and copies ran while one was open for 3% of the time, Pallas kernels for 0%

profile of v1, /device:TPU:264, one launch (start us, length us, event | category | flops | bytes accessed | tf_op | source)
XLA Modules:
  0.0 201.6 jit_solution(10169933083476981380)
XLA Ops:
  0.6 0.8 broadcast_in_dim.71
  1.5 49.9 %all_to_all.40 = bf16[16,24,768]{2,1,0:T(8,128)(2,1)S(1)} all-to-all(bf16[16,24,768]{2,1,0:T(8,128)(2,1)S(1)} %broadcast_in_dim.71), channel_id=1, replica_groups=mesh['x'=4,'zl'=6,'core'=2,'y'=8,'zh'=2] {'y','zh'}, dimensions={0} | all-to-all | bytes 1179648 | tf_op jit(solution)/shard_map/all_to_all | solution.py:25
  51.4 0.5 fusion.8
  51.9 1.1 convolution_convert_fusion
  53.0 0.3 pad_maximum_fusion
  53.4 4.9 %all_to_all.41 = f16[2,192,1920]{2,1,0:T(8,128)(2,1)S(1)} all-to-all(f16[2,192,1920]{2,1,0:T(8,128)(2,1)S(1)} %pad_maximum_fusion), channel_id=1, replica_groups=mesh['x'=4,'zl'=6,'core'=2,'y'=8,'zh'=2] {'core'}, dimensions={0} | all-to-all | bytes 2949120 | tf_op jit(solution)/shard_map/all_to_all | solution.py:25
  58.6 16.2 %all_to_all.42 = f16[4,48,1920]{2,1,0:T(8,128)(2,1)S(1)} all-to-all(f16[4,48,1920]{2,1,0:T(8,128)(2,1)S(1)} %bitcast.53), channel_id=1, replica_groups=mesh['x'=4,'zl'=6,'core'=2,'y'=8,'zh'=2] {'x'}, dimensions={0} | all-to-all | bytes 1474560 | tf_op jit(solution)/shard_map/all_to_all | solution.py:25
  74.9 0.7 convert_bitcast_fusion
  75.6 7.2 %all-to-all-start.3 = ((f16[6,8,1920]{2,1,0:T(8,128)(2,1)}), f16[6,8,1920]{2,1,0:T(8,128)(2,1)S(1)}, u32[]{:S(2)}, u32[]{:S(2)}) async-start(f16[6,8,1920]{2,1,0:T(8,128)(2,1)} %convert_bitcast_fusion), calls=%async_computation.3 | async-start | bytes 368640 | tf_op jit(solution)/shard_map/all_to_all | solution.py:25
  82.8 0.6 reduce_sum.102
  88.6 14.5 %all_to_all.43 = bf16[6,8,2432]{2,1,0:T(8,128)(2,1)S(1)} all-to-all(bf16[6,8,2432]{2,1,0:T(8,128)(2,1)S(1)} %broadcast_in_dim.75), channel_id=1, replica_groups=mesh['x'=4,'zl'=6,'core'=2,'y'=8,'zh'=2] {'zl'}, dimensions={0} | all-to-all | bytes 466944 | tf_op jit(solution)/shard_map/all_to_all | solution.py:25
  103.1 1.0 broadcast_in_dim.77
  104.1 3.5 %all-to-all-start.5 = ((bf16[4,48,2432]{2,1,0:T(8,128)(2,1)}), bf16[4,48,2432]{2,1,0:T(8,128)(2,1)S(1)}, u32[]{:S(2)}, u32[]{:S(2)}) async-start(bf16[4,48,2432]{2,1,0:T(8,128)(2,1)} %broadcast_in_dim.77), calls=%async_computation.5 | async-start | bytes 1867776 | tf_op jit(solution)/shard_map/all_to_all | solution.py:25
  107.7 13.3 %all-to-all-done.5 = bf16[4,48,2432]{2,1,0:T(8,128)(2,1)S(1)} async-done(((bf16[4,48,2432]{2,1,0:T(8,128)(2,1)}), bf16[4,48,2432]{2,1,0:T(8,128)(2,1)S(1)}, u32[]{:S(2)}, u32[]{:S(2)}) %all-to-all-start.5) | async-done | bytes 933920 | tf_op jit(solution)/shard_map/all_to_all | solution.py:25
  121.2 5.2 %all_to_all.44 = bf16[2,192,2432]{2,1,0:T(8,128)(2,1)S(1)} all-to-all(bf16[2,192,2432]{2,1,0:T(8,128)(2,1)S(1)} %broadcast_in_dim.79), channel_id=1, replica_groups=mesh['x'=4,'zl'=6,'core'=2,'y'=8,'zh'=2] {'core'}, dimensions={0} | all-to-all | bytes 3735552 | tf_op jit(solution)/shard_map/all_to_all | solution.py:25
  126.4 0.8 abs_reduce_fusion
  127.8 0.8 fusion.10
  128.6 0.8 fusion.6
  129.5 1.2 fusion.32
  133.9 3.6 %fusion = (f32[768]{0:T(1024)S(1)}, f32[1536,768]{1,0:T(8,128)}) fusion(bf16[384,768]{1,0:T(8,128)(2,1)S(1)} %bitcast.59, bf16[384,2432]{1,0:T(8,128)(2,1)S(1)} %bitcast.49), kind=kOutput, calls=%fused_computation.2 | convolution fusion | flops 908328192 | bytes 6491136 | tf_op jit(solution)/shard_map/dot_general | solution.py:82
  137.4 0.6 reduce_max.19
  138.8 2.8 %fusion.7 = f16[384,768]{1,0:T(8,128)(2,1)S(1)} fusion(bf16[768,1536]{1,0:T(8,128)(2,1)} %param.7, bf16[384,2432]{1,0:T(8,128)(2,1)S(1)} %bitcast.50, f32[]{:T(128)S(6)} %exp2.63), kind=kOutput, calls=%fused_computation.15 | convolution fusion | flops 906559488 | bytes 4128772 | tf_op jit(solution)/shard_map/dot_general | solution.py:85
  141.9 1.0 pad_maximum_fusion.1
  142.9 6.0 %all-to-all-start.7 = ((f16[16,24,896]{2,1,0:T(8,128)(2,1)}), f16[16,24,896]{2,1,0:T(8,128)(2,1)S(1)}, u32[]{:S(2)}, u32[]{:S(2)}) async-start(f16[16,24,896]{2,1,0:T(8,128)(2,1)} %pad_maximum_fusion.1), calls=%async_computation.7 | async-start | bytes 1376256 | tf_op jit(solution)/shard_map/all_to_all | solution.py:25
  148.9 4.3 %copy.23 = bf16[768,1536]{0,1:T(8,128)(2,1)} copy(bf16[768,1536]{1,0:T(8,128)(2,1)} %param.7) | data formatting | bytes 4718592 | tf_op args[2]
  153.2 0.6 convert_reduce_fusion.3
  154.6 35.6 %all-to-all-done.7 = f16[16,24,896]{2,1,0:T(8,128)(2,1)S(1)} async-done(((f16[16,24,896]{2,1,0:T(8,128)(2,1)}), f16[16,24,896]{2,1,0:T(8,128)(2,1)S(1)}, u32[]{:S(2)}, u32[]{:S(2)}) %all-to-all-start.7) | async-done | bytes 688160 | tf_op jit(solution)/shard_map/all_to_all | solution.py:25
  190.3 0.7 fusion.24
  191.1 0.8 fusion.9
  192.5 0.6 divide_sqrt_fusion
  193.1 4.2 %fusion.3 = bf16[768,1536]{0,1:T(8,128)(2,1)} fusion(f32[1536,768]{1,0:T(8,128)} %get-tuple-element.33, bf16[768,1536]{0,1:T(8,128)(2,1)S(1)} %copy-done, f32[1536]{0:T(1024)S(1)} %get-tuple-element.25, f32[768]{0:T(1024)S(1)} %get-tuple-element.23), kind=kLoop, calls=%fused_computation.5 | loop fusion | flops 8257536 | bytes 9446400 | tf_op jit(solution)/shard_map/convert_element_type | solution.py:116
  197.3 4.3 %copy.24 = bf16[768,1536]{1,0:T(8,128)(2,1)} copy(bf16[768,1536]{0,1:T(8,128)(2,1)} %fusion.3) | data formatting | bytes 4718592
  (36 shorter events, 1.4 us)
Async XLA Ops:
  1.4 50.5 %copy-start.1 = (bf16[768,1536]{1,0:T(8,128)(2,1)S(1)}, bf16[768,1536]{1,0:T(8,128)(2,1)}, u32[]{:S(2)}) copy-start(bf16[768,1536]{1,0:T(8,128)(2,1)} %param.7) | copy-start | bytes 7077892
  58.6 24.2 %copy-start.3 = (f32[768]{0:T(1024)S(1)}, f32[768]{0:T(1024)}, u32[]{:S(2)}) copy-start(f32[768]{0:T(1024)} %param.8) | copy-start | bytes 9220
  58.6 29.9 %copy-start.2 = (bf16[8,1536]{1,0:T(8,128)(2,1)S(1)}, bf16[8,1536]{1,0:T(8,128)(2,1)}, u32[]{:S(2)}) copy-start(bf16[8,1536]{1,0:T(8,128)(2,1)} %param.6) | copy-start | bytes 73732
  75.6 12.9 %all-to-all-start.3 = ((f16[6,8,1920]{2,1,0:T(8,128)(2,1)}), f16[6,8,1920]{2,1,0:T(8,128)(2,1)S(1)}, u32[]{:S(2)}, u32[]{:S(2)}) async-start(f16[6,8,1920]{2,1,0:T(8,128)(2,1)} %convert_bitcast_fusion), calls=%async_computation.3 | async-start | bytes 368640 | tf_op jit(solution)/shard_map/all_to_all | solution.py:25
  104.1 16.9 %all-to-all-start.5 = ((bf16[4,48,2432]{2,1,0:T(8,128)(2,1)}), bf16[4,48,2432]{2,1,0:T(8,128)(2,1)S(1)}, u32[]{:S(2)}, u32[]{:S(2)}) async-start(bf16[4,48,2432]{2,1,0:T(8,128)(2,1)} %broadcast_in_dim.77), calls=%async_computation.5 | async-start | bytes 1867776 | tf_op jit(solution)/shard_map/all_to_all | solution.py:25
  128.6 0.8 copy-start.4
  142.9 47.3 %all-to-all-start.7 = ((f16[16,24,896]{2,1,0:T(8,128)(2,1)}), f16[16,24,896]{2,1,0:T(8,128)(2,1)S(1)}, u32[]{:S(2)}, u32[]{:S(2)}) async-start(f16[16,24,896]{2,1,0:T(8,128)(2,1)} %pad_maximum_fusion.1), calls=%async_computation.7 | async-start | bytes 1376256 | tf_op jit(solution)/shard_map/all_to_all | solution.py:25
  153.2 40.0 %copy-start = (bf16[768,1536]{0,1:T(8,128)(2,1)S(1)}, bf16[768,1536]{0,1:T(8,128)(2,1)}, u32[]{:S(2)}) copy-start(bf16[768,1536]{0,1:T(8,128)(2,1)} %copy.23) | copy-start | bytes 7077892

commit v2 on v1

v2 whole, which is shorter than its diff:
```python
import jax
import jax.numpy as jnp
from jax import lax
from jax.experimental import pallas as pl
from jax.experimental.pallas import tpu as pltpu
from jax.sharding import Mesh
from jax.sharding import PartitionSpec as P

WIN = 36864
WOUT = 24576
ADAM_STEP = 10
WEIGHT_MAX = 0.03125
GRAM_SCALE = 1.0 / 32.0

X, ZL, CORE, Y, ZH = 4, 6, 2, 8, 2
ROWS = X * ZL * CORE
COLS = Y * ZH
f32, f16, bf16 = jnp.float32, jnp.float16, jnp.bfloat16


def silu_slope(preact):
    sig = jax.nn.sigmoid(preact)
    return sig * (1.0 + preact * (1.0 - sig))


def exchange(blocks, axis):
    return lax.all_to_all(blocks, axis, 0, 0)


def gather(block, axis, size):
    return exchange(jnp.broadcast_to(block[None], (size,) + block.shape), axis)


def exponent(bound):
    return jnp.ceil(jnp.log2(jnp.maximum(bound, 1e-30))) - 15.0


def split(value):
    high = lax.reduce_precision(value, 8, 7)
    return high.astype(bf16), value - high


def whole(value):
    return jnp.sum(jnp.sum(value, axis=0, keepdims=True), axis=1, keepdims=True)


NT = (((1,), (1,)), ((), ()))


def message_kernel(packed_ref, samples_ref, weight_ref, message_ref, partial_ref):
    batch, win = samples_ref.shape
    wout = weight_ref.shape[1]
    own = batch // COLS
    share = batch // ROWS
    slope = packed_ref[:, :wout]
    gram = packed_ref[:, wout : wout + batch].astype(f32) + packed_ref[:, wout + batch : wout + 2 * batch].astype(f32)
    partial_ref[...] = lax.dot_general(slope, weight_ref[...], NT, preferred_element_type=f32)
    mixed = lax.dot_general(slope, slope, NT, preferred_element_type=f32)
    total = whole(mixed * gram) * (1.0 / GRAM_SCALE)
    mixed_high = mixed.astype(bf16)
    mixed_low = (mixed - mixed_high.astype(f32)).astype(bf16)
    samples = samples_ref[...]
    spread = jnp.dot(mixed_high, samples, preferred_element_type=f32)
    spread += jnp.dot(mixed_low, samples, preferred_element_type=f32)
    row_total = jnp.sum(samples.astype(f32) * spread, axis=0, keepdims=True)

    top = jnp.max(jnp.max(jnp.abs(slope), axis=0, keepdims=True).astype(f32), axis=1, keepdims=True)
    grad_exp = exponent(top * (WEIGHT_MAX * wout))
    row_exp = exponent(jnp.max(row_total, axis=1, keepdims=True))
    total_exp = exponent(total)
    rows = row_total * jnp.exp2(-row_exp)
    rows = jnp.concatenate([rows[:, 128 * i : 128 * (i + 1)] for i in range(win // 128)], axis=0)
    rows_high = rows.astype(bf16).astype(f32)
    total = total * jnp.exp2(-total_exp)
    total_high = total.astype(bf16).astype(f32)
    lanes = lax.broadcasted_iota(jnp.int32, (1, 128), 1)
    scalars = jnp.zeros((1, 128), f32)
    for i, value in enumerate((grad_exp, row_exp, total_exp, total_high, (total - total_high) * 256.0)):
        scalars = jnp.where(lanes == i, value, scalars)
    pad = jnp.zeros((own - 2 * (win // 128) - 1, 128), f32)
    side = jnp.concatenate([rows_high, (rows - rows_high) * 256.0, scalars, pad], axis=0)
    factor = jnp.exp2(-grad_exp)
    each = own // share
    for dest in range(COLS):
        blocks = []
        for block in range(dest * each, (dest + 1) * each):
            first = ((block % CORE) * (ROWS // CORE) + block // CORE) * share
            blocks.append(partial_ref[first : first + share, :])
        message_ref[dest, :, :win] = jnp.concatenate(blocks, axis=0) * factor
        message_ref[dest, :, win:] = side


def make_message(packed, samples, weight):
    batch, win = samples.shape
    return pl.pallas_call(
        message_kernel,
        out_shape=jax.ShapeDtypeStruct((COLS, batch // COLS, win + 128), f32),
        in_specs=[pl.BlockSpec(memory_space=pltpu.VMEM)] * 3,
        out_specs=pl.BlockSpec(memory_space=pltpu.VMEM),
        scratch_shapes=[pltpu.VMEM((batch, win), f32)],
        compiler_params=pltpu.CompilerParams(vmem_limit_bytes=40 << 20),
    )(packed, samples, weight)


def update_kernel(message_ref, packed_ref, transposed_ref, weight_ref, row_second_ref, seconds_ref, col_root_ref,
                  input_grad_ref, new_row_ref, new_weight_ref, root_ref):
    win = row_second_ref.shape[1]
    wout = weight_ref.shape[1]
    groups = win // 128
    rows = weight_ref.shape[0]
    step = pl.program_id(0)

    @pl.when(step == 0)
    def _():
        total = jnp.zeros((1, 1), f32)
        sums = jnp.zeros((groups, 128), f32)
        grads = jnp.zeros(input_grad_ref.shape, f32)
        for source in range(COLS):
            side = message_ref[source, :, win:]
            scalars = side[2 * groups : 2 * groups + 1, :]
            powers = jnp.exp2(scalars[:, :3])
            grads += message_ref[source, :, :win] * powers[:, 0:1]
            sums += (side[:groups] + side[groups : 2 * groups] * (1.0 / 256.0)) * powers[:, 1:2]
            total += (scalars[:, 3:4] + scalars[:, 4:5] * (1.0 / 256.0)) * powers[:, 2:3]
        input_grad_ref[...] = grads.astype(bf16)
        row_total = jnp.concatenate([sums[i : i + 1] for i in range(groups)], axis=1)
        new_row = 0.999 * row_second_ref[...] + 0.001 * (row_total / WOUT)
        new_row_ref[...] = new_row
        scale = 0.999 * (seconds_ref[...] / WIN) + 0.001 * (total / WOUT / WIN)
        root = jnp.sqrt(new_row / (scale * (1.0 - 0.999**ADAM_STEP)))
        root_ref[...] = jnp.transpose(jnp.broadcast_to(root, (128, win)))

    grad = jnp.dot(transposed_ref[...], packed_ref[:, :wout], preferred_element_type=f32)
    root = root_ref[pl.ds(pl.multiple_of(step * rows, rows), rows), :]
    for i in range(0, wout, 128):
        bottom = root * col_root_ref[:, i : i + 128] + 1e-08
        change = 0.01 * grad[:, i : i + 128] / bottom
        new_weight_ref[:, i : i + 128] = (weight_ref[:, i : i + 128].astype(f32) - change).astype(bf16)


def update(message, packed, transposed, weight, row_second, seconds, col_root):
    win, wout = weight.shape
    rows = 256
    whole_in = [pl.BlockSpec(memory_space=pltpu.VMEM)]
    return pl.pallas_call(
        update_kernel,
        grid=(win // rows,),
        out_shape=(
            jax.ShapeDtypeStruct((message.shape[1], win), bf16),
            jax.ShapeDtypeStruct((1, win), f32),
            jax.ShapeDtypeStruct((win, wout), bf16),
        ),
        in_specs=whole_in * 2
        + [pl.BlockSpec((rows, transposed.shape[1]), lambda i: (i, 0)), pl.BlockSpec((rows, wout), lambda i: (i, 0))]
        + whole_in * 3,
        out_specs=(
            pl.BlockSpec((message.shape[1], win), lambda i: (0, 0)),
            pl.BlockSpec((1, win), lambda i: (0, 0)),
            pl.BlockSpec((rows, wout), lambda i: (i, 0)),
        ),
        scratch_shapes=[pltpu.VMEM((win, 128), f32)],
        compiler_params=pltpu.CompilerParams(vmem_limit_bytes=40 << 20),
    )(message, packed, transposed, weight, row_second[None], seconds, col_root)


def local(samples, cotangent, weight, row_second, col_second):
    own, win = samples.shape
    share, wout = cotangent.shape
    batch = own * COLS

    gathered = gather(samples, ("y", "zh"), COLS).reshape(X, ZL, CORE, share, win)
    gathered = gathered.transpose(2, 0, 1, 3, 4).reshape(batch, win)

    partial = jnp.dot(gathered, weight, preferred_element_type=f32)
    gram = lax.dot_general(gathered, gathered, (((1,), (1,)), ((), ())), preferred_element_type=f32)
    sums = jnp.concatenate([partial, gram * GRAM_SCALE], axis=1)
    for axis, size in (("core", CORE), ("x", X), ("zl", ZL)):
        blocks = sums.astype(f16).reshape(size, sums.shape[0] // size, sums.shape[1])
        sums = jnp.sum(exchange(blocks, axis).astype(f32), axis=0)
    slope = (cotangent.astype(f32) * silu_slope(sums[:, :wout])).astype(bf16)

    gram_high, gram_low = split(sums[:, wout:])
    second_one, rest = split(jnp.sum(row_second))
    second_two, second_three = split(rest)
    lanes = lax.broadcasted_iota(jnp.int32, (share, 128), 1)
    seconds = jnp.where(lanes == 0, second_one, jnp.where(lanes == 1, second_two, second_three.astype(bf16)))
    packed = jnp.concatenate([slope, gram_high, gram_low.astype(bf16), seconds], axis=1)
    for axis, size in (("zl", ZL), ("x", X), ("core", CORE)):
        packed = gather(packed, axis, size).reshape(packed.shape[0] * size, packed.shape[1])

    message = exchange(make_message(packed, gathered, weight).astype(f16), ("y", "zh")).astype(f32)

    slope = packed[:, :wout]
    mixed = jnp.dot(packed[:, wout : wout + batch], slope, preferred_element_type=f32)
    mixed += jnp.dot(packed[:, wout + batch : wout + 2 * batch], slope, preferred_element_type=f32)
    col_total = jnp.sum(slope.astype(f32) * mixed, axis=0) / GRAM_SCALE
    new_col = 0.999 * col_second + 0.001 * (col_total / WIN)
    seconds = packed.reshape(ROWS, share, -1)[:, 0, wout + 2 * batch :].astype(f32)
    seconds = jnp.sum(seconds[:, :3]).reshape(1, 1)
    input_grad, new_row, new_weight = update(
        message, packed, gathered.T, weight, row_second, seconds, jnp.sqrt(new_col)[None]
    )
    return (input_grad, new_weight, new_row[0], new_col)


def solution(mesh):
    fine = Mesh(mesh.devices.reshape(X, ZL, CORE, Y, ZH), ("x", "zl", "core", "y", "zh"))
    row, col = ("x", "zl", "core"), ("y", "zh")
    in_specs = (P(col, row), P(row, col), P(row, col), P(row), P(col))
    out_specs = (P(col, row), P(row, col), P(row), P(col))
    return jax.shard_map(local, mesh=fine, in_specs=in_specs, out_specs=out_specs, check_vma=False)
```

time: 203 us -> 185 us (0.911)
  blocking collectives: 90.7 us -> 107 us
  waiting for transfers between devices: 49.1 us -> 38.2 us
  local copies, waits for them, and re-layouts: 10.8 us -> 3.08 us
  Pallas kernels: 0 us -> 7.71 us
  other arithmetic: 12.9 us -> 6.08 us
  matrix products: 9.48 us -> 3.16 us
  between operations: 11.9 us -> 5.78 us
  starting transfers between devices: 16.7 us -> 13.2 us
    all_to_all x5 -> x6, blocking collectives: 90.7 us -> 107 us  [exchange(): return lax.all_to_all(blocks, axis, 0, 0)]
    all_to_all x3 -> x2, waiting for transfers between devices: 49.1 us -> 38.2 us  [exchange(): return lax.all_to_all(blocks, axis, 0, 0)]
    pallas_call x0 -> x2, Pallas kernels: none -> 7.71 us  [the longest x1 4.14 us: update(): pl.pallas_call(update_kernel, grid=(win // rows,), out_shape=(jax.ShapeDt...]
    unnamed x13, local copies, waits for them, and re-layouts: 8.57 us -> 1.7 us
    dot_general x4 -> x2, matrix products: 7.91 us -> 1.59 us  [the longest x1 0.83 us: local(): jnp.dot(packed[:, wout + batch:wout + 2 * batch], slope, preferred_elemen...]
    all_to_all x3 -> x2, starting transfers between devices: 16.7 us -> 13.2 us  [exchange(): return lax.all_to_all(blocks, axis, 0, 0)]
    convert_element_type x4 -> x3, other arithmetic: 4.27 us -> 2.12 us  [the longest x1 1.19 us: local(): exchange(make_message(packed, gathered, weight).astype(f16), ('y', 'zh'))]
  transfers between devices with their start and end apart: 3 -> 2, of which waited for: 3 -> 2; matrix products, arithmetic and copies ran while one was open for 3% -> 2% of each run, Pallas kernels for 0% -> 0%
where the time goes in v2:
time: 185 us; the launch traced here: 184 us
  blocking collectives  107 us (58%)
  waiting for transfers between devices  38.2 us (21%)
  starting transfers between devices  13.2 us (7%)
  Pallas kernels  7.71 us (4%)
  other arithmetic  6.08 us (3%)
  between operations  5.78 us (3%)
  matrix products  3.16 us (2%)
  local copies, waits for them, and re-layouts  3.08 us (2%)
    all_to_all x6, blocking collectives, exchange(): return lax.all_to_all(blocks, axis, 0, 0)  107 us
    all_to_all x2, waiting for transfers between devices, exchange(): return lax.all_to_all(blocks, axis, 0, 0)  38.2 us
    all_to_all x2, starting transfers between devices, exchange(): return lax.all_to_all(blocks, axis, 0, 0)  13.2 us
    pallas_call x1, Pallas kernels, update(): pl.pallas_call(update_kernel, grid=(win // rows,), out_shape=(jax.ShapeDt...  4.14 us
  transfers between devices with their start and end apart: 2, of which 2 were waited for; matrix products, arithmetic and copies ran while one was open for 2% of the time, Pallas kernels for 0%

profile of v2, /device:TPU:264, one launch (start us, length us, event | category | flops | bytes accessed | tf_op | source)
XLA Modules:
  0.0 183.9 jit_solution(6365223094615868194)
XLA Ops:
  0.6 0.8 broadcast_in_dim.44
  1.5 49.9 %all_to_all.40 = bf16[16,24,768]{2,1,0:T(8,128)(2,1)S(1)} all-to-all(bf16[16,24,768]{2,1,0:T(8,128)(2,1)S(1)} %broadcast_in_dim.44), channel_id=1, replica_groups=mesh['x'=4,'zl'=6,'core'=2,'y'=8,'zh'=2] {'y','zh'}, dimensions={0} | all-to-all | bytes 1179648 | tf_op jit(solution)/shard_map/all_to_all | solution.py:27
  51.4 0.5 fusion.3
  51.9 1.1 convolution_convert_fusion
  53.0 0.3 pad_maximum_fusion
  53.4 4.9 %all_to_all.41 = f16[2,192,1920]{2,1,0:T(8,128)(2,1)S(1)} all-to-all(f16[2,192,1920]{2,1,0:T(8,128)(2,1)S(1)} %pad_maximum_fusion), channel_id=1, replica_groups=mesh['x'=4,'zl'=6,'core'=2,'y'=8,'zh'=2] {'core'}, dimensions={0} | all-to-all | bytes 2949120 | tf_op jit(solution)/shard_map/all_to_all | solution.py:27
  58.3 0.3 convert_reduce_fusion
  58.5 0.1 convert_element_type.61
  58.6 16.2 %all_to_all.42 = f16[4,48,1920]{2,1,0:T(8,128)(2,1)S(1)} all-to-all(f16[4,48,1920]{2,1,0:T(8,128)(2,1)S(1)} %bitcast.35), channel_id=1, replica_groups=mesh['x'=4,'zl'=6,'core'=2,'y'=8,'zh'=2] {'x'}, dimensions={0} | all-to-all | bytes 1474560 | tf_op jit(solution)/shard_map/all_to_all | solution.py:27
  74.8 0.1 convert_reduce_fusion.1
  74.9 0.7 convert_bitcast_fusion
  75.6 7.2 %all-to-all-start.3 = ((f16[6,8,1920]{2,1,0:T(8,128)(2,1)}), f16[6,8,1920]{2,1,0:T(8,128)(2,1)S(1)}, u32[]{:S(2)}, u32[]{:S(2)}) async-start(f16[6,8,1920]{2,1,0:T(8,128)(2,1)} %convert_bitcast_fusion), calls=%async_computation.3 | async-start | bytes 368640 | tf_op jit(solution)/shard_map/all_to_all | solution.py:27
  82.8 0.6 reduce_sum.57
  88.4 0.1 all-to-all-done.3
  88.6 14.5 %all_to_all.43 = bf16[6,8,2432]{2,1,0:T(8,128)(2,1)S(1)} all-to-all(bf16[6,8,2432]{2,1,0:T(8,128)(2,1)S(1)} %broadcast_in_dim.48), channel_id=1, replica_groups=mesh['x'=4,'zl'=6,'core'=2,'y'=8,'zh'=2] {'zl'}, dimensions={0} | all-to-all | bytes 466944 | tf_op jit(solution)/shard_map/all_to_all | solution.py:27
  103.1 0.1 broadcast_in_dim.50
  103.2 15.8 %all_to_all.44 = bf16[4,48,2432]{2,1,0:T(8,128)(2,1)S(1)} all-to-all(bf16[4,48,2432]{2,1,0:T(8,128)(2,1)S(1)} %broadcast_in_dim.50), channel_id=1, replica_groups=mesh['x'=4,'zl'=6,'core'=2,'y'=8,'zh'=2] {'x'}, dimensions={0} | all-to-all | bytes 1867776 | tf_op jit(solution)/shard_map/all_to_all | solution.py:27
  119.0 0.1 broadcast_in_dim.52
  119.2 5.3 %all_to_all.45 = bf16[2,192,2432]{2,1,0:T(8,128)(2,1)S(1)} all-to-all(bf16[2,192,2432]{2,1,0:T(8,128)(2,1)S(1)} %broadcast_in_dim.52), channel_id=1, replica_groups=mesh['x'=4,'zl'=6,'core'=2,'y'=8,'zh'=2] {'core'}, dimensions={0} | all-to-all | bytes 3735552 | tf_op jit(solution)/shard_map/all_to_all | solution.py:27
  124.5 3.6 %shard_map.84 = f32[16,24,896]{2,1,0:T(8,128)S(1)} custom-call(bf16[384,2432]{1,0:T(8,128)(2,1)S(1)} %bitcast.24, bf16[384,768]{1,0:T(8,128)(2,1)S(1)} %bitcast.31, bf16[768,1536]{1,0:T(8,128)(2,1)S(1)} %copy-done.1), custom_call_target="tpu_custom_call" | custom-call | tf_op jit(solution)/shard_map/pallas_call | solution.py:95
  128.1 0.9 convert_element_type.73
  129.0 6.0 %all-to-all-start.7 = ((f16[16,24,896]{2,1,0:T(8,128)(2,1)}), f16[16,24,896]{2,1,0:T(8,128)(2,1)}, u32[]{:S(2)}, u32[]{:S(2)}) async-start(f16[16,24,896]{2,1,0:T(8,128)(2,1)} %convert_element_type.73), calls=%async_computation.7 | async-start | bytes 1376256 | tf_op jit(solution)/shard_map/all_to_all | solution.py:27
  135.0 0.3 copy.19
  135.4 0.8 fusion.4
  136.2 0.8 fusion.2
  137.0 0.6 fusion.10
  137.6 0.6 convert_reduce_fusion.3
  138.2 38.1 %all-to-all-done.7 = f16[16,24,896]{2,1,0:T(8,128)(2,1)} async-done(((f16[16,24,896]{2,1,0:T(8,128)(2,1)}), f16[16,24,896]{2,1,0:T(8,128)(2,1)}, u32[]{:S(2)}, u32[]{:S(2)}) %all-to-all-start.7) | async-done | bytes 688160 | tf_op jit(solution)/shard_map/all_to_all | solution.py:27
  176.3 1.2 convert_element_type.74.message_ref
  177.5 1.7 copy-done.2
  179.2 4.1 %shard_map.85 = (bf16[24,768]{1,0:T(8,128)(2,1)}, f32[1,768]{1,0:T(1,128)S(1)}, bf16[768,1536]{1,0:T(8,128)(2,1)}) custom-call(f32[16,24,896]{2,1,0:T(8,128)S(1)} %convert_element_type.74.message_ref, bf16[384,2432]{1,0:T(8,128)(2,1)S(1)} %bitcast.28, bf16[768,384]{1,0:T(8,128)(2,1)S(1)} %bitcast.33, bf16[768,1536]{1,0:T(8,128)(2,1)S(1)} %copy-done.2, ...), custom_call_target="tpu_custom_call" | custom-call | tf_op jit(solution)/shard_map/pallas_call | solution.py:145
  183.3 0.6 reduce
  (24 shorter events, 0.2 us)
Async XLA Ops:
  1.4 50.5 %copy-start = (bf16[768,1536]{1,0:T(8,128)(2,1)S(1)}, bf16[768,1536]{1,0:T(8,128)(2,1)}, u32[]{:S(2)}) copy-start(bf16[768,1536]{1,0:T(8,128)(2,1)} %weight_ref.3) | copy-start | bytes 7077892
  58.6 24.2 %copy-start.4 = (f32[768]{0:T(1024)S(1)}, f32[768]{0:T(1024)}, u32[]{:S(2)}) copy-start(f32[768]{0:T(1024)} %param.8) | copy-start | bytes 9220
  58.6 29.9 %copy-start.3 = (bf16[8,1536]{1,0:T(8,128)(2,1)S(1)}, bf16[8,1536]{1,0:T(8,128)(2,1)}, u32[]{:S(2)}) copy-start(bf16[8,1536]{1,0:T(8,128)(2,1)} %param.6) | copy-start | bytes 73732
  75.6 12.9 %all-to-all-start.3 = ((f16[6,8,1920]{2,1,0:T(8,128)(2,1)}), f16[6,8,1920]{2,1,0:T(8,128)(2,1)S(1)}, u32[]{:S(2)}, u32[]{:S(2)}) async-start(f16[6,8,1920]{2,1,0:T(8,128)(2,1)} %convert_bitcast_fusion), calls=%async_computation.3 | async-start | bytes 368640 | tf_op jit(solution)/shard_map/all_to_all | solution.py:27
  119.1 5.4 %copy-start.1 = (bf16[768,1536]{1,0:T(8,128)(2,1)S(1)}, bf16[768,1536]{1,0:T(8,128)(2,1)}, u32[]{:S(2)}) copy-start(bf16[768,1536]{1,0:T(8,128)(2,1)} %weight_ref.3) | copy-start | bytes 7077892
  129.0 47.3 %all-to-all-start.7 = ((f16[16,24,896]{2,1,0:T(8,128)(2,1)}), f16[16,24,896]{2,1,0:T(8,128)(2,1)}, u32[]{:S(2)}, u32[]{:S(2)}) async-start(f16[16,24,896]{2,1,0:T(8,128)(2,1)} %convert_element_type.73), calls=%async_computation.7 | async-start | bytes 1376256 | tf_op jit(solution)/shard_map/all_to_all | solution.py:27
  136.2 0.9 copy-start.5
  177.5 1.7 copy-start.2

commit v3 on v2

v3 whole, which is shorter than its diff:
```python
import jax
import jax.numpy as jnp
from jax import lax
from jax.experimental import pallas as pl
from jax.experimental.pallas import tpu as pltpu
from jax.sharding import Mesh
from jax.sharding import PartitionSpec as P

WIN = 36864
WOUT = 24576
ADAM_STEP = 10
WEIGHT_MAX = 0.03125
GRAM_SCALE = 1.0 / 32.0

X, ZL, CORE, Y, ZH = 4, 6, 2, 8, 2
ROWS = X * ZL * CORE
COLS = Y * ZH
f32, f16, bf16 = jnp.float32, jnp.float16, jnp.bfloat16


def silu_slope(preact):
    sig = jax.nn.sigmoid(preact)
    return sig * (1.0 + preact * (1.0 - sig))


def exchange(blocks, axis):
    return lax.all_to_all(blocks, axis, 0, 0)


def gather(block, axis, size):
    return exchange(jnp.broadcast_to(block[None], (size,) + block.shape), axis)


def exponent(bound):
    return jnp.ceil(jnp.log2(jnp.maximum(bound, 1e-30))) - 15.0


def split(value):
    high = lax.reduce_precision(value, 8, 7)
    return high.astype(bf16), value - high


def whole(value):
    return jnp.sum(jnp.sum(value, axis=0, keepdims=True), axis=1, keepdims=True)


NT = (((1,), (1,)), ((), ()))


def halves(batch):
    return batch // 2 + batch // ROWS


def pack_kernel(place_ref, sums_ref, cotangent_ref, row_second_ref, packed_ref):
    share, wout = cotangent_ref.shape
    batch = sums_ref.shape[1] - wout
    side = packed_ref.shape[1] - wout
    count = halves(batch)
    packed_ref[:, :wout] = (cotangent_ref[...].astype(f32) * silu_slope(sums_ref[:, :wout])).astype(bf16)
    shift = lax.rem(batch - place_ref[0] * share, batch)
    gram = pltpu.roll(sums_ref[:, wout:], shift, 1)
    gram = jnp.concatenate([gram, jnp.zeros((share, side - batch), f32)], axis=1)
    high = gram.astype(bf16).astype(f32)
    low = pltpu.roll(gram - high, count, 1)
    lanes = lax.broadcasted_iota(jnp.int32, (share, side), 1)
    out = jnp.where(lanes < count, high, jnp.where(lanes < 2 * count, low, 0.0))
    rest = whole(row_second_ref[...])
    for i in range(3):
        part = rest.astype(bf16).astype(f32)
        rest = rest - part
        out = jnp.where(lanes == 2 * count + i, part, out)
    packed_ref[:, wout:] = out.astype(bf16)


def pack(place, sums, cotangent, row_second):
    share, wout = cotangent.shape
    width = wout + -(-(2 * halves(sums.shape[1] - wout) + 3) // 128) * 128
    return pl.pallas_call(
        pack_kernel,
        out_shape=jax.ShapeDtypeStruct((share, width), bf16),
        in_specs=[pl.BlockSpec(memory_space=pltpu.SMEM)] + [pl.BlockSpec(memory_space=pltpu.VMEM)] * 3,
        out_specs=pl.BlockSpec(memory_space=pltpu.VMEM),
        compiler_params=pltpu.CompilerParams(vmem_limit_bytes=16 << 20),
    )(place, sums, cotangent, row_second)


def message_kernel(packed_ref, samples_ref, weight_ref, message_ref, gram_ref, partial_ref):
    batch, win = samples_ref.shape
    wout = weight_ref.shape[1]
    own = batch // COLS
    share = batch // ROWS
    slope = packed_ref[:, :wout]
    count = halves(batch)
    lanes = lax.broadcasted_iota(jnp.int32, (share, batch), 1)
    times = jnp.where(lanes < share, 1.0, jnp.where(lanes < batch // 2, 2.0, jnp.where(lanes < count, 1.0, 0.0)))
    packed_half = packed_ref[:, wout:].astype(f32)
    for place in range(ROWS):
        half = packed_half[place * share : (place + 1) * share, :]
        half = half + pltpu.roll(half, half.shape[1] - count, 1)
        gram_ref[place * share : (place + 1) * share, :] = pltpu.roll(half[:, :batch] * times, place * share, 1)
    gram = gram_ref[...]
    partial_ref[...] = lax.dot_general(slope, weight_ref[...], NT, preferred_element_type=f32)
    mixed = lax.dot_general(slope, slope, NT, preferred_element_type=f32)
    total = whole(mixed * gram) * (1.0 / GRAM_SCALE)
    mixed_high = mixed.astype(bf16)
    mixed_low = (mixed - mixed_high.astype(f32)).astype(bf16)
    samples = samples_ref[...]
    spread = jnp.dot(mixed_high, samples, preferred_element_type=f32)
    spread += jnp.dot(mixed_low, samples, preferred_element_type=f32)
    row_total = jnp.sum(samples.astype(f32) * spread, axis=0, keepdims=True)

    top = jnp.max(jnp.max(jnp.abs(slope), axis=0, keepdims=True).astype(f32), axis=1, keepdims=True)
    grad_exp = exponent(top * (WEIGHT_MAX * wout))
    row_exp = exponent(jnp.max(row_total, axis=1, keepdims=True))
    total_exp = exponent(total)
    rows = row_total * jnp.exp2(-row_exp)
    rows = jnp.concatenate([rows[:, 128 * i : 128 * (i + 1)] for i in range(win // 128)], axis=0)
    rows_high = rows.astype(bf16).astype(f32)
    total = total * jnp.exp2(-total_exp)
    total_high = total.astype(bf16).astype(f32)
    lanes = lax.broadcasted_iota(jnp.int32, (1, 128), 1)
    scalars = jnp.zeros((1, 128), f32)
    for i, value in enumerate((grad_exp, row_exp, total_exp, total_high, (total - total_high) * 256.0)):
        scalars = jnp.where(lanes == i, value, scalars)
    pad = jnp.zeros((own - 2 * (win // 128) - 1, 128), f32)
    side = jnp.concatenate([rows_high, (rows - rows_high) * 256.0, scalars, pad], axis=0)
    factor = jnp.exp2(-grad_exp)
    each = own // share
    for dest in range(COLS):
        blocks = []
        for block in range(dest * each, (dest + 1) * each):
            first = ((block % CORE) * (ROWS // CORE) + block // CORE) * share
            blocks.append(partial_ref[first : first + share, :])
        message_ref[dest, :, :win] = jnp.concatenate(blocks, axis=0) * factor
        message_ref[dest, :, win:] = side


def make_message(packed, samples, weight):
    batch, win = samples.shape
    return pl.pallas_call(
        message_kernel,
        out_shape=(
            jax.ShapeDtypeStruct((COLS, batch // COLS, win + 128), f32),
            jax.ShapeDtypeStruct((batch, batch), f32),
        ),
        in_specs=[pl.BlockSpec(memory_space=pltpu.VMEM)] * 3,
        out_specs=(pl.BlockSpec(memory_space=pltpu.VMEM),) * 2,
        scratch_shapes=[pltpu.VMEM((batch, win), f32)],
        compiler_params=pltpu.CompilerParams(vmem_limit_bytes=20 << 20),
    )(packed, samples, weight)


CHUNKS = 3


def update_kernel(message_ref, packed_ref, transposed_ref, weight_ref, row_second_ref, seconds_ref, col_root_ref,
                  input_grad_ref, new_row_ref, new_weight_ref, root_ref, old_ref, new_ref, old_sems, new_sems):
    win, wout = old_ref.shape
    groups = win // 128
    rows = win // CHUNKS

    def fetch(i):
        part = pl.ds(i * rows, rows)
        return pltpu.make_async_copy(weight_ref.at[part], old_ref.at[part], old_sems.at[i])

    def store(i):
        part = pl.ds(i * rows, rows)
        return pltpu.make_async_copy(new_ref.at[part], new_weight_ref.at[part], new_sems.at[i])

    for i in range(CHUNKS):
        fetch(i).start()
    total = jnp.zeros((1, 1), f32)
    sums = jnp.zeros((groups, 128), f32)
    grads = jnp.zeros(input_grad_ref.shape, f32)
    for source in range(COLS):
        side = message_ref[source, :, win:]
        scalars = side[2 * groups : 2 * groups + 1, :]
        powers = jnp.exp2(scalars[:, :3])
        grads += message_ref[source, :, :win] * powers[:, 0:1]
        sums += (side[:groups] + side[groups : 2 * groups] * (1.0 / 256.0)) * powers[:, 1:2]
        total += (scalars[:, 3:4] + scalars[:, 4:5] * (1.0 / 256.0)) * powers[:, 2:3]
    input_grad_ref[...] = grads.astype(bf16)
    new_row = 0.999 * row_second_ref[...] + 0.001 * (sums / WOUT)
    new_row_ref[...] = new_row
    scale = 0.999 * (seconds_ref[...] / WIN) + 0.001 * (total / WOUT / WIN)
    root = jnp.sqrt(new_row / (scale * (1.0 - 0.999**ADAM_STEP)))
    for i in range(groups):
        root_ref[128 * i : 128 * (i + 1), :] = jnp.transpose(jnp.broadcast_to(root[i : i + 1], (128, 128)))

    for i in range(CHUNKS):
        part = slice(i * rows, (i + 1) * rows)
        grad = jnp.dot(transposed_ref[part, :], packed_ref[:, :wout], preferred_element_type=f32)
        root = root_ref[part, :]
        fetch(i).wait()
        for j in range(0, wout, 128):
            bottom = root * col_root_ref[:, j : j + 128] + 1e-08
            change = 0.01 * grad[:, j : j + 128] / bottom
            new_ref[part, j : j + 128] = (old_ref[part, j : j + 128].astype(f32) - change).astype(bf16)
        store(i).start()
    for i in range(CHUNKS):
        store(i).wait()


def update(message, packed, transposed, weight, row_second, seconds, col_root):
    win, wout = weight.shape
    inside, outside = pl.BlockSpec(memory_space=pltpu.VMEM), pl.BlockSpec(memory_space=pltpu.HBM)
    return pl.pallas_call(
        update_kernel,
        out_shape=(
            jax.ShapeDtypeStruct((message.shape[1], win), bf16),
            jax.ShapeDtypeStruct((win // 128, 128), f32),
            jax.ShapeDtypeStruct((win, wout), bf16),
        ),
        in_specs=[inside, inside, inside, outside, inside, inside, inside],
        out_specs=(inside, inside, outside),
        scratch_shapes=[
            pltpu.VMEM((win, 128), f32),
            pltpu.VMEM((win, wout), bf16),
            pltpu.VMEM((win, wout), bf16),
            pltpu.SemaphoreType.DMA((CHUNKS,)),
            pltpu.SemaphoreType.DMA((CHUNKS,)),
        ],
        compiler_params=pltpu.CompilerParams(vmem_limit_bytes=24 << 20),
    )(message, packed, transposed, weight, row_second.reshape(-1, 128), seconds, col_root)


def local(samples, cotangent, weight, row_second, col_second):
    own, win = samples.shape
    share, wout = cotangent.shape
    batch = own * COLS

    gathered = gather(samples, ("y", "zh"), COLS).reshape(X, ZL, CORE, share, win)
    gathered = gathered.transpose(2, 0, 1, 3, 4).reshape(batch, win)

    partial = jnp.dot(gathered, weight, preferred_element_type=f32)
    gram = lax.dot_general(gathered, gathered, (((1,), (1,)), ((), ())), preferred_element_type=f32)
    sums = jnp.concatenate([partial, gram * GRAM_SCALE], axis=1)
    for axis, size in (("core", CORE), ("x", X), ("zl", ZL)):
        blocks = sums.astype(f16).reshape(size, sums.shape[0] // size, sums.shape[1])
        sums = jnp.sum(exchange(blocks, axis).astype(f32), axis=0)

    place = (lax.axis_index("core") * X + lax.axis_index("x")) * ZL + lax.axis_index("zl")
    packed = pack(place.astype(jnp.int32)[None], sums, cotangent, row_second.reshape(-1, 128))
    for axis, size in (("zl", ZL), ("x", X), ("core", CORE)):
        packed = gather(packed, axis, size).reshape(packed.shape[0] * size, packed.shape[1])

    message, gram = make_message(packed, gathered, weight)
    message = exchange(message.astype(f16), ("y", "zh")).astype(f32)

    slope = packed[:, :wout]
    gram_high, gram_low = split(gram)
    mixed = jnp.dot(gram_high, slope, preferred_element_type=f32)
    mixed += jnp.dot(gram_low.astype(bf16), slope, preferred_element_type=f32)
    col_total = jnp.sum(slope.astype(f32) * mixed, axis=0) / GRAM_SCALE
    new_col = 0.999 * col_second + 0.001 * (col_total / WIN)
    seconds = packed.reshape(ROWS, share, -1)[:, 0, wout + 2 * halves(batch) :].astype(f32)
    seconds = jnp.sum(seconds[:, :3]).reshape(1, 1)
    input_grad, new_row, new_weight = update(
        message, packed, gathered.T, weight, row_second, seconds, jnp.sqrt(new_col)[None]
    )
    return (input_grad, new_weight, new_row.reshape(win), new_col)


def solution(mesh):
    fine = Mesh(mesh.devices.reshape(X, ZL, CORE, Y, ZH), ("x", "zl", "core", "y", "zh"))
    row, col = ("x", "zl", "core"), ("y", "zh")
    in_specs = (P(col, row), P(row, col), P(row, col), P(row), P(col))
    out_specs = (P(col, row), P(row, col), P(row), P(col))
    return jax.shard_map(local, mesh=fine, in_specs=in_specs, out_specs=out_specs, check_vma=False)
```

time: 185 us -> 183 us (0.989)
  waiting for transfers between devices: 38.2 us -> 44.8 us
  blocking collectives: 107 us -> 101 us
  between operations: 5.78 us -> 0.81 us
    all_to_all x2, waiting for transfers between devices: 38.2 us -> 44.8 us  [exchange(): return lax.all_to_all(blocks, axis, 0, 0)]
    all_to_all x6, blocking collectives: 107 us -> 101 us  [exchange(): return lax.all_to_all(blocks, axis, 0, 0)]
    pallas_call x2 -> x3, Pallas kernels: 7.71 us -> 9.15 us  [the longest x1 5.33 us: update(): pl.pallas_call(update_kernel, out_shape=(jax.ShapeDtypeStruct((message.sh...]
where the time goes in v3:
time: 183 us; the launch traced here: 182 us
  blocking collectives  101 us (55%)
  waiting for transfers between devices  44.8 us (24%)
  starting transfers between devices  14.5 us (8%)
  Pallas kernels  9.15 us (5%)
  other arithmetic  4.85 us (3%)
  local copies, waits for them, and re-layouts  4.33 us (2%)
  matrix products  3.19 us (2%)
    all_to_all x6, blocking collectives, exchange(): return lax.all_to_all(blocks, axis, 0, 0)  101 us
    all_to_all x2, waiting for transfers between devices, exchange(): return lax.all_to_all(blocks, axis, 0, 0)  44.8 us
    all_to_all x2, starting transfers between devices, exchange(): return lax.all_to_all(blocks, axis, 0, 0)  14.5 us
    pallas_call x1, Pallas kernels, update(): pl.pallas_call(update_kernel, out_shape=(jax.ShapeDtypeStruct((message.sh...  5.33 us
  transfers between devices with their start and end apart: 2, of which 2 were waited for; matrix products, arithmetic and copies ran while one was open for 2% of the time, Pallas kernels for 0%

profile of v3, /device:TPU:264, one launch (start us, length us, event | category | flops | bytes accessed | tf_op | source)
XLA Modules:
  0.0 182.2 jit_solution(3724016332431295133)
XLA Ops:
  0.6 0.8 broadcast_in_dim.33
  1.4 49.8 %all_to_all.40 = bf16[16,24,768]{2,1,0:T(8,128)(2,1)S(1)} all-to-all(bf16[16,24,768]{2,1,0:T(8,128)(2,1)S(1)} %broadcast_in_dim.33), channel_id=1, replica_groups=mesh['x'=4,'zl'=6,'core'=2,'y'=8,'zh'=2] {'y','zh'}, dimensions={0} | all-to-all | bytes 1179648 | tf_op jit(solution)/shard_map/all_to_all | solution.py:27
  51.3 0.5 fusion.3
  51.8 1.1 copy-done
  52.9 1.1 convolution_convert_fusion
  54.0 0.3 pad_maximum_fusion
  54.4 4.9 %all_to_all.41 = f16[2,192,1920]{2,1,0:T(8,128)(2,1)S(1)} all-to-all(f16[2,192,1920]{2,1,0:T(8,128)(2,1)S(1)} %pad_maximum_fusion), channel_id=1, replica_groups=mesh['x'=4,'zl'=6,'core'=2,'y'=8,'zh'=2] {'core'}, dimensions={0} | all-to-all | bytes 2949120 | tf_op jit(solution)/shard_map/all_to_all | solution.py:27
  59.3 0.3 convert_reduce_fusion
  59.5 0.1 convert_element_type.45
  59.6 16.2 %all_to_all.42 = f16[4,48,1920]{2,1,0:T(8,128)(2,1)S(1)} all-to-all(f16[4,48,1920]{2,1,0:T(8,128)(2,1)S(1)} %bitcast.40), channel_id=1, replica_groups=mesh['x'=4,'zl'=6,'core'=2,'y'=8,'zh'=2] {'x'}, dimensions={0} | all-to-all | bytes 1474560 | tf_op jit(solution)/shard_map/all_to_all | solution.py:27
  75.8 0.1 convert_reduce_fusion.1
  75.9 0.7 convert_bitcast_fusion
  76.6 7.2 %all-to-all-start.3 = ((f16[6,8,1920]{2,1,0:T(8,128)(2,1)}), f16[6,8,1920]{2,1,0:T(8,128)(2,1)S(1)}, u32[]{:S(2)}, u32[]{:S(2)}) async-start(f16[6,8,1920]{2,1,0:T(8,128)(2,1)} %convert_bitcast_fusion), calls=%async_computation.3 | async-start | bytes 368640 | tf_op jit(solution)/shard_map/all_to_all | solution.py:27
  83.8 5.7 %all-to-all-done.3 = f16[6,8,1920]{2,1,0:T(8,128)(2,1)S(1)} async-done(((f16[6,8,1920]{2,1,0:T(8,128)(2,1)}), f16[6,8,1920]{2,1,0:T(8,128)(2,1)S(1)}, u32[]{:S(2)}, u32[]{:S(2)}) %all-to-all-start.3) | async-done | bytes 184352 | tf_op jit(solution)/shard_map/all_to_all | solution.py:27
  89.5 0.2 shard_map.84
  89.7 12.7 %all_to_all.43 = bf16[6,8,2048]{2,1,0:T(8,128)(2,1)S(1)} all-to-all(bf16[6,8,2048]{2,1,0:T(8,128)(2,1)S(1)} %broadcast_in_dim.34), channel_id=1, replica_groups=mesh['x'=4,'zl'=6,'core'=2,'y'=8,'zh'=2] {'zl'}, dimensions={0} | all-to-all | bytes 393216 | tf_op jit(solution)/shard_map/all_to_all | solution.py:27
  102.5 11.9 %all_to_all.44 = bf16[4,48,2048]{2,1,0:T(8,128)(2,1)S(1)} all-to-all(bf16[4,48,2048]{2,1,0:T(8,128)(2,1)S(1)} %broadcast_in_dim.36), channel_id=1, replica_groups=mesh['x'=4,'zl'=6,'core'=2,'y'=8,'zh'=2] {'x'}, dimensions={0} | all-to-all | bytes 1572864 | tf_op jit(solution)/shard_map/all_to_all | solution.py:27
  114.4 0.2 broadcast_in_dim.38
  114.5 5.1 %all_to_all.45 = bf16[2,192,2048]{2,1,0:T(8,128)(2,1)S(1)} all-to-all(bf16[2,192,2048]{2,1,0:T(8,128)(2,1)S(1)} %broadcast_in_dim.38), channel_id=1, replica_groups=mesh['x'=4,'zl'=6,'core'=2,'y'=8,'zh'=2] {'core'}, dimensions={0} | all-to-all | bytes 3145728 | tf_op jit(solution)/shard_map/all_to_all | solution.py:27
  119.7 3.6 %shard_map.85 = (f32[16,24,896]{2,1,0:T(8,128)S(1)}, f32[384,384]{1,0:T(8,128)S(1)}) custom-call(bf16[384,2048]{1,0:T(8,128)(2,1)S(1)} %bitcast.27, bf16[384,768]{1,0:T(8,128)(2,1)S(1)} %bitcast.34, bf16[768,1536]{1,0:T(8,128)(2,1)S(1)} %copy-done.1), custom_call_target="tpu_custom_call" | custom-call | tf_op jit(solution)/shard_map/pallas_call | solution.py:140
  123.3 0.9 convert_element_type.51
  124.3 7.3 %all-to-all-start.7 = ((f16[16,24,896]{2,1,0:T(8,128)(2,1)}), f16[16,24,896]{2,1,0:T(8,128)(2,1)}, u32[]{:S(2)}, u32[]{:S(2)}) async-start(f16[16,24,896]{2,1,0:T(8,128)(2,1)} %convert_element_type.51), calls=%async_computation.7 | async-start | bytes 1376256 | tf_op jit(solution)/shard_map/all_to_all | solution.py:27
  131.5 0.3 copy.19
  131.8 0.8 fusion.4
  132.6 0.8 fusion.2
  133.5 0.6 fusion.9
  134.1 0.1 slice.16
  134.2 0.6 convert_reduce_fusion.3
  134.9 39.2 %all-to-all-done.7 = f16[16,24,896]{2,1,0:T(8,128)(2,1)} async-done(((f16[16,24,896]{2,1,0:T(8,128)(2,1)}), f16[16,24,896]{2,1,0:T(8,128)(2,1)}, u32[]{:S(2)}, u32[]{:S(2)}) %all-to-all-start.7) | async-done | bytes 688160 | tf_op jit(solution)/shard_map/all_to_all | solution.py:27
  174.0 1.2 convert_element_type.52.message_ref
  175.2 1.7 copy-done.2
  176.9 5.3 %shard_map.86 = (bf16[24,768]{1,0:T(8,128)(2,1)}, f32[6,128]{1,0:T(8,128)}, bf16[768,1536]{1,0:T(8,128)(2,1)}) custom-call(f32[16,24,896]{2,1,0:T(8,128)S(1)} %convert_element_type.52.message_ref, bf16[384,2048]{1,0:T(8,128)(2,1)S(1)} %bitcast.31, bf16[768,384]{1,0:T(8,128)(2,1)S(1)} %bitcast.36, bf16[768,1536]{1,0:T(8,128)(2,1)S(1)} %copy-done.2, ...), custom_call_target="tpu_custom_call" | custom-call | tf_op jit(solution)/shard_map/pallas_call | solution.py:207
  (16 shorter events, 0.2 us)
Async XLA Ops:
  51.3 1.7 copy-start
  59.6 29.9 %copy-start.3 = (bf16[8,1536]{1,0:T(8,128)(2,1)S(1)}, bf16[8,1536]{1,0:T(8,128)(2,1)}, u32[]{:S(2)}) copy-start(bf16[8,1536]{1,0:T(8,128)(2,1)} %cotangent_ref.1) | copy-start | bytes 73732
  59.6 29.9 %copy-start.4 = (f32[768]{0:T(1024)S(1)}, f32[768]{0:T(1024)}, u32[]{:S(2)}) copy-start(f32[768]{0:T(1024)} %param.8) | copy-start | bytes 9220
  76.6 12.9 %all-to-all-start.3 = ((f16[6,8,1920]{2,1,0:T(8,128)(2,1)}), f16[6,8,1920]{2,1,0:T(8,128)(2,1)S(1)}, u32[]{:S(2)}, u32[]{:S(2)}) async-start(f16[6,8,1920]{2,1,0:T(8,128)(2,1)} %convert_bitcast_fusion), calls=%async_computation.3 | async-start | bytes 368640 | tf_op jit(solution)/shard_map/all_to_all | solution.py:27
  114.5 5.1 %copy-start.1 = (bf16[768,1536]{1,0:T(8,128)(2,1)S(1)}, bf16[768,1536]{1,0:T(8,128)(2,1)}, u32[]{:S(2)}) copy-start(bf16[768,1536]{1,0:T(8,128)(2,1)} %weight_ref.3) | copy-start | bytes 7077892
  124.3 49.8 %all-to-all-start.7 = ((f16[16,24,896]{2,1,0:T(8,128)(2,1)}), f16[16,24,896]{2,1,0:T(8,128)(2,1)}, u32[]{:S(2)}, u32[]{:S(2)}) async-start(f16[16,24,896]{2,1,0:T(8,128)(2,1)} %convert_element_type.51), calls=%async_computation.7 | async-start | bytes 1376256 | tf_op jit(solution)/shard_map/all_to_all | solution.py:27
  132.6 0.9 copy-start.5
  175.2 1.7 copy-start.2

commit v4 on v3

v4 whole, which is shorter than its diff:
```python
import jax
import jax.numpy as jnp
from jax import lax
from jax.experimental import pallas as pl
from jax.experimental.pallas import tpu as pltpu
from jax.sharding import Mesh
from jax.sharding import PartitionSpec as P

WIN = 36864
WOUT = 24576
ADAM_STEP = 10
WEIGHT_MAX = 0.03125
GRAM_SCALE = 1.0 / 32.0

X, ZL, CORE, Y, ZH = 4, 6, 2, 8, 2
ROWS = X * ZL * CORE
COLS = Y * ZH
f32, f16, bf16 = jnp.float32, jnp.float16, jnp.bfloat16


def silu_slope(preact):
    sig = jax.nn.sigmoid(preact)
    return sig * (1.0 + preact * (1.0 - sig))


def exchange(blocks, axis):
    return lax.all_to_all(blocks, axis, 0, 0)


def gather(block, axis, size):
    return exchange(jnp.broadcast_to(block[None], (size,) + block.shape), axis)


def exponent(bound):
    return jnp.ceil(jnp.log2(jnp.maximum(bound, 1e-30))) - 15.0


def split(value):
    high = lax.reduce_precision(value, 8, 7)
    return high.astype(bf16), value - high


def whole(value):
    return jnp.sum(jnp.sum(value, axis=0, keepdims=True), axis=1, keepdims=True)


def encode(own, grad_exp, rows, total):
    row_exp = exponent(jnp.max(jnp.max(rows, axis=0, keepdims=True), axis=1, keepdims=True))
    total_exp = exponent(total)
    rows = rows * jnp.exp2(-row_exp)
    rows_high = rows.astype(bf16).astype(f32)
    total = total * jnp.exp2(-total_exp)
    total_high = total.astype(bf16).astype(f32)
    lanes = lax.broadcasted_iota(jnp.int32, (1, 128), 1)
    scalars = jnp.zeros((1, 128), f32)
    for i, value in enumerate((grad_exp, row_exp, total_exp, total_high, (total - total_high) * 256.0)):
        scalars = jnp.where(lanes == i, value, scalars)
    pad = jnp.zeros((own - 2 * rows.shape[0] - 1, 128), f32)
    return jnp.concatenate([rows_high, (rows - rows_high) * 256.0, scalars, pad], axis=0)


NT = (((1,), (1,)), ((), ()))


def halves(batch):
    return batch // 2 + batch // ROWS


def pack_kernel(place_ref, sums_ref, cotangent_ref, row_second_ref, packed_ref):
    share, wout = cotangent_ref.shape
    batch = sums_ref.shape[1] - wout
    side = packed_ref.shape[1] - wout
    count = halves(batch)
    packed_ref[:, :wout] = (cotangent_ref[...].astype(f32) * silu_slope(sums_ref[:, :wout])).astype(bf16)
    shift = lax.rem(batch - place_ref[0] * share, batch)
    gram = pltpu.roll(sums_ref[:, wout:], shift, 1)
    gram = jnp.concatenate([gram, jnp.zeros((share, side - batch), f32)], axis=1)
    high = gram.astype(bf16).astype(f32)
    low = pltpu.roll(gram - high, count, 1)
    lanes = lax.broadcasted_iota(jnp.int32, (share, side), 1)
    out = jnp.where(lanes < count, high, jnp.where(lanes < 2 * count, low, 0.0))
    rest = whole(row_second_ref[...])
    for i in range(3):
        part = rest.astype(bf16).astype(f32)
        rest = rest - part
        out = jnp.where(lanes == 2 * count + i, part, out)
    packed_ref[:, wout:] = out.astype(bf16)


def pack(place, sums, cotangent, row_second):
    share, wout = cotangent.shape
    width = wout + -(-(2 * halves(sums.shape[1] - wout) + 3) // 128) * 128
    return pl.pallas_call(
        pack_kernel,
        out_shape=jax.ShapeDtypeStruct((share, width), bf16),
        in_specs=[pl.BlockSpec(memory_space=pltpu.SMEM)] + [pl.BlockSpec(memory_space=pltpu.VMEM)] * 3,
        out_specs=pl.BlockSpec(memory_space=pltpu.VMEM),
        compiler_params=pltpu.CompilerParams(vmem_limit_bytes=16 << 20),
    )(place, sums, cotangent, row_second)


def message_kernel(core_ref, mine_ref, other_ref, samples_ref, weight_ref,
                   message_ref, seconds_ref, slope_ref, gram_ref, partial_ref):
    batch, win = samples_ref.shape
    wout = weight_ref.shape[1]
    own = batch // COLS
    share = batch // ROWS
    half = batch // CORE
    first = core_ref[0] == 0
    packed_half = []
    for i, (low, high) in enumerate(((mine_ref, other_ref), (other_ref, mine_ref))):
        both = jnp.where(first, low[...], high[...])
        slope_ref[i * half : (i + 1) * half, :] = both[:, :wout]
        packed_half.append(both[:, wout:].astype(f32))
    packed_half = jnp.concatenate(packed_half, axis=0)
    slope = slope_ref[...]
    partial_ref[...] = lax.dot_general(slope, weight_ref[...], NT, preferred_element_type=f32)
    count = halves(batch)
    lanes = lax.broadcasted_iota(jnp.int32, packed_half.shape, 1)
    there = (lanes >= 2 * count) & (lanes < 2 * count + 3)
    seconds_ref[...] = whole(jnp.where(there, packed_half, 0.0)) * (1.0 / share)
    lanes = lax.broadcasted_iota(jnp.int32, (share, batch), 1)
    times = jnp.where(lanes < share, 1.0, jnp.where(lanes < batch // 2, 2.0, jnp.where(lanes < count, 1.0, 0.0)))
    for place in range(ROWS):
        piece = packed_half[place * share : (place + 1) * share, :]
        piece = piece + pltpu.roll(piece, piece.shape[1] - count, 1)
        gram_ref[place * share : (place + 1) * share, :] = pltpu.roll(piece[:, :batch] * times, place * share, 1)
    gram = gram_ref[...]
    partial_ref[...] = lax.dot_general(slope, weight_ref[...], NT, preferred_element_type=f32)
    mixed = lax.dot_general(slope, slope, NT, preferred_element_type=f32)
    total = whole(mixed * gram) * (1.0 / GRAM_SCALE)
    mixed_high = mixed.astype(bf16)
    mixed_low = (mixed - mixed_high.astype(f32)).astype(bf16)
    samples = samples_ref[...]
    spread = jnp.dot(mixed_high, samples, preferred_element_type=f32)
    spread += jnp.dot(mixed_low, samples, preferred_element_type=f32)
    row_total = jnp.sum(samples.astype(f32) * spread, axis=0, keepdims=True)

    top = jnp.max(jnp.max(jnp.abs(slope), axis=0, keepdims=True).astype(f32), axis=1, keepdims=True)
    grad_exp = exponent(top * (WEIGHT_MAX * wout))
    rows = jnp.concatenate([row_total[:, 128 * i : 128 * (i + 1)] for i in range(win // 128)], axis=0)
    side = encode(own, grad_exp, rows, total)
    factor = jnp.exp2(-grad_exp)
    each = own // share
    for dest in range(COLS):
        blocks = []
        for block in range(dest * each, (dest + 1) * each):
            start = ((block % CORE) * (ROWS // CORE) + block // CORE) * share
            blocks.append(partial_ref[start : start + share, :])
        message_ref[dest, :, :win] = jnp.concatenate(blocks, axis=0) * factor
        message_ref[dest, :, win:] = side


INSIDE, OUTSIDE = pl.BlockSpec(memory_space=pltpu.VMEM), pl.BlockSpec(memory_space=pltpu.HBM)
SCALAR = pl.BlockSpec(memory_space=pltpu.SMEM)


def make_message(core, mine, other, samples, weight):
    batch, win = samples.shape
    return pl.pallas_call(
        message_kernel,
        out_shape=(
            jax.ShapeDtypeStruct((COLS, batch // COLS, win + 128), f32),
            jax.ShapeDtypeStruct((1, 1), f32),
            jax.ShapeDtypeStruct((batch, weight.shape[1]), bf16),
            jax.ShapeDtypeStruct((batch, batch), f32),
        ),
        in_specs=[SCALAR] + [INSIDE] * 4,
        out_specs=(INSIDE,) * 4,
        scratch_shapes=[pltpu.VMEM((batch, win), f32)],
        compiler_params=pltpu.CompilerParams(vmem_limit_bytes=20 << 20),
    )(core, mine, other, samples, weight)


def decode(pieces):
    own, width = pieces[0].shape
    win = width - 128
    groups = win // 128
    scalars = jnp.concatenate([piece[2 * groups : 2 * groups + 1, win:] for piece in pieces], axis=0)
    powers = jnp.exp2(scalars)
    grads = jnp.zeros((own, win), f32)
    sums = jnp.zeros((groups, 128), f32)
    for i, piece in enumerate(pieces):
        grads += piece[:, :win] * powers[i : i + 1, 0:1]
        side = piece[: 2 * groups, win:]
        sums += (side[:groups] + side[groups:] * (1.0 / 256.0)) * powers[i : i + 1, 1:2]
    total = whole((scalars[:, 3:4] + scalars[:, 4:5] * (1.0 / 256.0)) * powers[:, 2:3])
    return grads, sums, total, jnp.max(scalars[:, 0:1], axis=0, keepdims=True)


def decode_kernel(zh_ref, message_ref, keep_ref, send_ref):
    zh = zh_ref[0]
    grads, sums, total, _ = decode([message_ref[i, zh] for i in range(Y)])
    own, win = grads.shape
    keep_ref[:, :win] = grads
    lanes = lax.broadcasted_iota(jnp.int32, (1, 128), 1)
    rows = [sums, jnp.where(lanes == 0, total, 0.0), jnp.zeros((own - sums.shape[0] - 1, 128), f32)]
    keep_ref[:, win:] = jnp.concatenate(rows, axis=0)
    grads, sums, total, grad_exp = decode([message_ref[i, 1 - zh] for i in range(Y)])
    grad_exp += 3.0
    send_ref[:, :win] = grads * jnp.exp2(-grad_exp)
    send_ref[:, win:] = encode(own, grad_exp, sums, total)


def decoded(zh, message):
    return pl.pallas_call(
        decode_kernel,
        out_shape=(jax.ShapeDtypeStruct(message.shape[2:], f32),) * 2,
        in_specs=[SCALAR, INSIDE],
        out_specs=(INSIDE,) * 2,
        compiler_params=pltpu.CompilerParams(vmem_limit_bytes=12 << 20),
    )(zh, message)


CHUNKS = 3


def grad_kernel(transposed_ref, slope_ref, weight_ref, grad_ref, old_ref):
    rows = grad_ref.shape[0] // CHUNKS
    for i in range(CHUNKS):
        part = slice(i * rows, (i + 1) * rows)
        grad_ref[part, :] = jnp.dot(transposed_ref[part, :], slope_ref[...], preferred_element_type=f32)
        old_ref[part, :] = weight_ref[part, :]


def make_grad(transposed, slope, weight):
    return pl.pallas_call(
        grad_kernel,
        out_shape=(jax.ShapeDtypeStruct(weight.shape, f32), jax.ShapeDtypeStruct(weight.shape, bf16)),
        in_specs=[INSIDE] * 3,
        out_specs=(INSIDE,) * 2,
        compiler_params=pltpu.CompilerParams(vmem_limit_bytes=20 << 20),
    )(transposed, slope, weight)


def update_kernel(keep_ref, received_ref, grad_ref, old_ref, row_second_ref, seconds_ref, col_root_ref,
                  input_grad_ref, new_row_ref, new_weight_ref, root_ref, new_ref, sems):
    win, wout = old_ref.shape
    groups = win // 128
    rows = win // CHUNKS

    def store(i):
        part = pl.ds(i * rows, rows)
        return pltpu.make_async_copy(new_ref.at[part], new_weight_ref.at[part], sems.at[i])

    grads, sums, total, _ = decode([received_ref[...]])
    input_grad_ref[...] = (grads + keep_ref[:, :win]).astype(bf16)
    sums += keep_ref[:groups, win:]
    total += keep_ref[groups : groups + 1, win : win + 1]
    new_row = 0.999 * row_second_ref[...] + 0.001 * (sums / WOUT)
    new_row_ref[...] = new_row
    scale = 0.999 * (seconds_ref[...] / WIN) + 0.001 * (total / WOUT / WIN)
    root = 100.0 * jnp.sqrt(new_row / (scale * (1.0 - 0.999**ADAM_STEP)))
    for i in range(groups):
        root_ref[128 * i : 128 * (i + 1), :] = jnp.transpose(jnp.broadcast_to(root[i : i + 1], (128, 128)))

    for i in range(CHUNKS):
        part = slice(i * rows, (i + 1) * rows)
        root = root_ref[part, :]
        for j in range(0, wout, 128):
            bottom = root * col_root_ref[:, j : j + 128] + 1e-06
            change = grad_ref[part, j : j + 128] / bottom
            new_ref[part, j : j + 128] = (old_ref[part, j : j + 128].astype(f32) - change).astype(bf16)
        store(i).start()
    for i in range(CHUNKS):
        store(i).wait()


def update(keep, received, grad, weight, row_second, seconds, col_root):
    win, wout = weight.shape
    return pl.pallas_call(
        update_kernel,
        out_shape=(
            jax.ShapeDtypeStruct((keep.shape[0], win), bf16),
            jax.ShapeDtypeStruct((win // 128, 128), f32),
            jax.ShapeDtypeStruct((win, wout), bf16),
        ),
        in_specs=[INSIDE] * 7,
        out_specs=(INSIDE, INSIDE, OUTSIDE),
        scratch_shapes=[
            pltpu.VMEM((win, 128), f32),
            pltpu.VMEM((win, wout), bf16),
            pltpu.SemaphoreType.DMA((CHUNKS,)),
        ],
        compiler_params=pltpu.CompilerParams(vmem_limit_bytes=20 << 20),
    )(keep, received, grad, weight, row_second.reshape(-1, 128), seconds, col_root)


SWAP = ((0, 1), (1, 0))


def local(samples, cotangent, weight, row_second, col_second):
    own, win = samples.shape
    share, wout = cotangent.shape
    batch = own * COLS
    core, zh = lax.axis_index("core").astype(jnp.int32), lax.axis_index("zh").astype(jnp.int32)
    place = ((core * X + lax.axis_index("x")) * ZL + lax.axis_index("zl")).astype(jnp.int32)
    samples, core, zh, place, first = lax.optimization_barrier((samples, core, zh, place, core == 0))

    near = lax.all_gather(samples, "zh", axis=0, tiled=True)
    gathered = gather(near, "y", Y).reshape(X, ZL, CORE, share, win).transpose(2, 0, 1, 3, 4)
    mine = jnp.where(first, gathered[0], gathered[1]).reshape(batch // CORE, win)
    theirs = jnp.where(first, gathered[1], gathered[0]).reshape(batch // CORE, win)
    gathered = gathered.reshape(batch, win)

    def partial(rows):
        gram = lax.dot_general(rows, gathered, NT, preferred_element_type=f32)
        return jnp.concatenate([jnp.dot(rows, weight, preferred_element_type=f32), gram * GRAM_SCALE], axis=1)

    sums = lax.ppermute(partial(theirs).astype(f16), "core", SWAP).astype(f32) + partial(mine)
    for axis, size in (("x", X), ("zl", ZL)):
        blocks = sums.astype(f16).reshape(size, sums.shape[0] // size, sums.shape[1])
        sums = jnp.sum(exchange(blocks, axis).astype(f32), axis=0)

    packed = pack(place[None], sums, cotangent, row_second.reshape(-1, 128))
    for axis, size in (("zl", ZL), ("x", X)):
        packed = gather(packed, axis, size).reshape(packed.shape[0] * size, packed.shape[1])
    other = lax.ppermute(packed, "core", SWAP)

    message, seconds, slope, gram = make_message(core[None], packed, other, gathered, weight)
    message = exchange(message.astype(f16).reshape(Y, ZH, own, win + 128), "y").astype(f32)
    message, slope, gram, gathered = lax.optimization_barrier((message, slope, gram, gathered))
    keep, send = decoded(zh[None], message)
    received = lax.ppermute(send.astype(f16), "zh", SWAP).astype(f32)

    gram_high, gram_low = split(gram)
    mixed = jnp.dot(gram_high, slope, preferred_element_type=f32)
    mixed += jnp.dot(gram_low.astype(bf16), slope, preferred_element_type=f32)
    col_total = jnp.sum(slope.astype(f32) * mixed, axis=0) / GRAM_SCALE
    new_col = 0.999 * col_second + 0.001 * (col_total / WIN)
    grad, old = make_grad(gathered.T, slope, weight)
    input_grad, new_row, new_weight = update(
        keep, received, grad, old, row_second, seconds, jnp.sqrt(new_col)[None]
    )
    return (input_grad, new_weight, new_row.reshape(win), new_col)


def solution(mesh):
    fine = Mesh(mesh.devices.reshape(X, ZL, CORE, Y, ZH), ("x", "zl", "core", "y", "zh"))
    row, col = ("x", "zl", "core"), ("y", "zh")
    in_specs = (P(col, row), P(row, col), P(row, col), P(row), P(col))
    out_specs = (P(col, row), P(row, col), P(row), P(col))
    return jax.shard_map(local, mesh=fine, in_specs=in_specs, out_specs=out_specs, check_vma=False)
```

time: 183 us -> 162 us (0.89)
  the two profiles are of different devices: /device:TPU:264 before, /device:TPU:1 now
where the time goes in v4:
time: 162 us
  blocking collectives  117 us (72%)
  starting transfers between devices  21.5 us (13%)
  Pallas kernels  10.1 us (6%)
  matrix products  3.58 us (2%)
  local copies, waits for them, and re-layouts  2.96 us (2%)
  other arithmetic  2.75 us (2%)
  waiting for transfers between devices  2.7 us (2%)
    all_to_all x6, blocking collectives, exchange(): return lax.all_to_all(blocks, axis, 0, 0)  101 us
    all_gather x1, blocking collectives, local(): near = lax.all_gather(samples, 'zh', axis=0, tiled=True)  16.1 us
    ppermute x1, starting transfers between devices, local(): received = lax.ppermute(send.astype(f16), 'zh', SWAP).astype(f32)  8.48 us
    ppermute x1, starting transfers between devices, local(): other = lax.ppermute(packed, 'core', SWAP)  7.17 us
    ppermute x1, starting transfers between devices, local(): lax.ppermute(partial(theirs).astype(f16), 'core', SWAP).astype(f32)  5.84 us
    pallas_call x1, Pallas kernels, make_message(): pl.pallas_call(message_kernel, out_shape=(jax.ShapeDtypeStruct((COLS, bat...  4.74 us
    pallas_call x1, Pallas kernels, update(): pl.pallas_call(update_kernel, out_shape=(jax.ShapeDtypeStruct((keep.shape...  3.51 us
  transfers between devices with their start and end apart: 3, of which 2 were waited for; matrix products, arithmetic and copies ran while one was open for 2% of the time, Pallas kernels for 1%

profile of v4, /device:TPU:1, one launch (start us, length us, event | category | flops | bytes accessed | tf_op | source)
XLA Modules:
  0.0 161.7 jit_solution(15200320347466404526)
XLA Ops:
  0.6 16.1 %all_gather.3 = bf16[48,768]{1,0:T(8,128)(2,1)S(1)} all-gather(bf16[24,768]{1,0:T(8,128)(2,1)} %param.5), channel_id=1, replica_groups=mesh['x'=4,'zl'=6,'core'=2,'y'=8,'zh'=2] {'zh'}, dimensions={0}, use_global_device_ids=true | all-gather | bytes 110592 | tf_op jit(solution)/shard_map/all_gather | solution.py:300
  16.8 22.5 %all_to_all.30 = bf16[8,48,768]{2,1,0:T(8,128)(2,1)S(1)} all-to-all(bf16[8,48,768]{2,1,0:T(8,128)(2,1)S(1)} %broadcast_in_dim.34), channel_id=1, replica_groups=mesh['x'=4,'zl'=6,'core'=2,'y'=8,'zh'=2] {'y'}, dimensions={0} | all-to-all | bytes 1179648 | tf_op jit(solution)/shard_map/all_to_all | solution.py:27
  39.4 0.4 fusion.3
  39.8 1.2 copy-done
  41.0 0.6 convolution_convert_fusion
  41.6 0.2 pad_maximum_fusion
  41.8 5.8 %collective-permute-start = (f16[192,1920]{1,0:T(8,128)(2,1)S(1)}, f16[192,1920]{1,0:T(8,128)(2,1)S(1)}, u32[]{:S(2)}, u32[]{:S(2)}) collective-permute-start(f16[192,1920]{1,0:T(8,128)(2,1)S(1)} %pad_maximum_fusion), channel_id=1, source_target_pairs={{0,16},{16,0},{1,17},{17,1},{2,18},{18,2},{3,19},{19,3},{4,20},{20... | collective-permute-start | bytes 2211848 | tf_op jit(solution)/shard_map/ppermute | solution.py:310
  47.6 0.4 convolution_multiply_fusion
  48.0 0.6 fusion.8
  48.6 0.8 collective-permute-done
  49.5 0.2 fusion.1
  49.6 15.0 %all_to_all.31 = f16[4,48,1920]{2,1,0:T(8,128)(2,1)S(1)} all-to-all(f16[4,48,1920]{2,1,0:T(8,128)(2,1)S(1)} %bitcast.41), channel_id=1, replica_groups=mesh['x'=4,'zl'=6,'core'=2,'y'=8,'zh'=2] {'x'}, dimensions={0} | all-to-all | bytes 1474560 | tf_op jit(solution)/shard_map/all_to_all | solution.py:27
  64.6 0.1 convert_reduce_fusion
  64.7 16.9 %all_to_all.32 = f16[6,8,1920]{2,1,0:T(8,128)(2,1)S(1)} all-to-all(f16[6,8,1920]{2,1,0:T(8,128)(2,1)S(1)} %convert_bitcast_fusion), channel_id=1, replica_groups=mesh['x'=4,'zl'=6,'core'=2,'y'=8,'zh'=2] {'zl'}, dimensions={0} | all-to-all | bytes 368640 | tf_op jit(solution)/shard_map/all_to_all | solution.py:27
  81.7 0.2 shard_map.84
  81.8 12.2 %all_to_all.33 = bf16[6,8,2048]{2,1,0:T(8,128)(2,1)S(1)} all-to-all(bf16[6,8,2048]{2,1,0:T(8,128)(2,1)S(1)} %broadcast_in_dim.35), channel_id=1, replica_groups=mesh['x'=4,'zl'=6,'core'=2,'y'=8,'zh'=2] {'zl'}, dimensions={0} | all-to-all | bytes 393216 | tf_op jit(solution)/shard_map/all_to_all | solution.py:27
  94.1 10.7 %all_to_all.34 = bf16[4,48,2048]{2,1,0:T(8,128)(2,1)S(1)} all-to-all(bf16[4,48,2048]{2,1,0:T(8,128)(2,1)S(1)} %broadcast_in_dim.37), channel_id=1, replica_groups=mesh['x'=4,'zl'=6,'core'=2,'y'=8,'zh'=2] {'x'}, dimensions={0} | all-to-all | bytes 1572864 | tf_op jit(solution)/shard_map/all_to_all | solution.py:27
  104.9 7.2 %collective-permute-start.1 = (bf16[192,2048]{1,0:T(8,128)(2,1)S(1)}, bf16[192,2048]{1,0:T(8,128)(2,1)S(1)}, u32[]{:S(2)}, u32[]{:S(2)}) collective-permute-start(bf16[192,2048]{1,0:T(8,128)(2,1)S(1)} %bitcast.32), channel_id=1, source_target_pairs={{0,16},{16,0},{1,17},{17,1},{2,18},{18,2},{3,19},{19,3},{4,20},{20... | collective-permute-start | bytes 2359304 | tf_op jit(solution)/shard_map/ppermute | solution.py:318
  112.1 1.9 %collective-permute-done.1.other_ref = bf16[192,2048]{1,0:T(8,128)(2,1)S(1)} collective-permute-done((bf16[192,2048]{1,0:T(8,128)(2,1)S(1)}, bf16[192,2048]{1,0:T(8,128)(2,1)S(1)}, u32[]{:S(2)}, u32[]{:S(2)}) %collective-permute-start.1) | collective-permute-done | bytes 786464 | tf_op jit(solution)/shard_map/ppermute | solution.py:318
  114.0 4.7 %shard_map.85 = (f32[16,24,896]{2,1,0:T(8,128)S(1)}, f32[1,1]{1,0:T(1,128)}, bf16[384,1536]{1,0:T(8,128)(2,1)S(1)}, f32[384,384]{1,0:T(8,128)S(1)}) custom-call(s32[1]{0:T(128)} %bitcast.1.core_ref, bf16[192,2048]{1,0:T(8,128)(2,1)S(1)} %bitcast.33, bf16[192,2048]{1,0:T(8,128)(2,1)S(1)} %collective-permute-done.1.other_ref, bf16[384,768]{1,0:T(8,128)(2,1)S(1)} %bitcast.30, ...), custom_call_target="tpu_custom_call" | custom-call | tf_op jit(solution)/shard_map/pallas_call | solution.py:160
  118.8 23.9 %all_to_all.35 = f16[8,2,24,896]{3,2,1,0:T(8,128)(2,1)S(1)} all-to-all(f16[8,2,24,896]{3,2,1,0:T(8,128)(2,1)S(1)} %bitcast.42), channel_id=1, replica_groups=mesh['x'=4,'zl'=6,'core'=2,'y'=8,'zh'=2] {'y'}, dimensions={0} | all-to-all | bytes 1376256 | tf_op jit(solution)/shard_map/all_to_all | solution.py:27
  142.8 0.3 shard_map.86
  143.1 0.6 convert_element_type.49
  143.7 8.5 %collective-permute-start.2 = (f16[24,896]{1,0:T(8,128)(2,1)}, f16[24,896]{1,0:T(8,128)(2,1)}, u32[]{:S(2)}, u32[]{:S(2)}) collective-permute-start(f16[24,896]{1,0:T(8,128)(2,1)} %convert_element_type.49), channel_id=1, source_target_pairs={{0,1},{1,0},{2,3},{3,2},{4,5},{5,4},{6,7},{7,6},{8,9},{9,8},{10,11... | collective-permute-start | bytes 129032 | tf_op jit(solution)/shard_map/ppermute | solution.py:324
  152.2 0.8 fusion.6
  153.0 0.8 fusion.2
  153.8 0.6 fusion.7
  154.4 0.3 copy.13
  154.8 1.3 copy-done.2
  156.0 1.4 shard_map.87
  157.4 0.8 convert_element_type.50.received_ref
  158.2 3.5 %shard_map.88 = (bf16[24,768]{1,0:T(8,128)(2,1)}, f32[6,128]{1,0:T(8,128)}, bf16[768,1536]{1,0:T(8,128)(2,1)}) custom-call(f32[24,896]{1,0:T(8,128)S(1)} %copy-done.4, f32[24,896]{1,0:T(8,128)S(1)} %convert_element_type.50.received_ref, f32[768,1536]{1,0:T(8,128)S(1)} %get-tuple-element.37.grad_ref, bf16[768,1536]{1,0:T(8,128)(2,1)S(1)} %get-tuple-element.38.old_ref, ...), custom_call_target="tpu_custom_call" | custom-call | tf_op jit(solution)/shard_map/pallas_call | solution.py:271
  (25 shorter events, 0.5 us)
Async XLA Ops:
  39.3 1.7 %copy-start = (bf16[768,1536]{1,0:T(8,128)(2,1)S(1)}, bf16[768,1536]{1,0:T(8,128)(2,1)}, u32[]{:S(2)}) copy-start(bf16[768,1536]{1,0:T(8,128)(2,1)} %weight_ref.3) | copy-start | bytes 7077892
  41.8 7.7 %collective-permute-start = (f16[192,1920]{1,0:T(8,128)(2,1)S(1)}, f16[192,1920]{1,0:T(8,128)(2,1)S(1)}, u32[]{:S(2)}, u32[]{:S(2)}) collective-permute-start(f16[192,1920]{1,0:T(8,128)(2,1)S(1)} %pad_maximum_fusion), channel_id=1, source_target_pairs={{0,16},{16,0},{1,17},{17,1},{2,18},{18,2},{3,19},{19,3},{4,20},{20... | collective-permute-start | bytes 2211848 | tf_op jit(solution)/shard_map/ppermute | solution.py:310
  64.6 17.0 %copy-start.5 = (bf16[8,1536]{1,0:T(8,128)(2,1)S(1)}, bf16[8,1536]{1,0:T(8,128)(2,1)}, u32[]{:S(2)}) copy-start(bf16[8,1536]{1,0:T(8,128)(2,1)} %cotangent_ref.1) | copy-start | bytes 73732
  64.6 17.0 %copy-start.6 = (f32[768]{0:T(1024)S(1)}, f32[768]{0:T(1024)}, u32[]{:S(2)}) copy-start(f32[768]{0:T(1024)} %param.8) | copy-start | bytes 9220
  104.9 9.1 %collective-permute-start.1 = (bf16[192,2048]{1,0:T(8,128)(2,1)S(1)}, bf16[192,2048]{1,0:T(8,128)(2,1)S(1)}, u32[]{:S(2)}, u32[]{:S(2)}) collective-permute-start(bf16[192,2048]{1,0:T(8,128)(2,1)S(1)} %bitcast.32), channel_id=1, source_target_pairs={{0,16},{16,0},{1,17},{17,1},{2,18},{18,2},{3,19},{19,3},{4,20},{20... | collective-permute-start | bytes 2359304 | tf_op jit(solution)/shard_map/ppermute | solution.py:318
  118.7 34.3 %copy-start.1 = (bf16[384,1536]{1,0:T(8,128)(2,1)}, bf16[384,1536]{1,0:T(8,128)(2,1)S(1)}, u32[]{:S(2)}) copy-start(bf16[384,1536]{1,0:T(8,128)(2,1)S(1)} %get-tuple-element.36.slope_ref) | copy-start | bytes 3538948
  143.1 0.7 copy-start.3
  143.7 13.7 %collective-permute-start.2 = (f16[24,896]{1,0:T(8,128)(2,1)}, f16[24,896]{1,0:T(8,128)(2,1)}, u32[]{:S(2)}, u32[]{:S(2)}) collective-permute-start(f16[24,896]{1,0:T(8,128)(2,1)} %convert_element_type.49), channel_id=1, source_target_pairs={{0,1},{1,0},{2,3},{3,2},{4,5},{5,4},{6,7},{7,6},{8,9},{9,8},{10,11... | collective-permute-start | bytes 129032 | tf_op jit(solution)/shard_map/ppermute | solution.py:324
  153.0 0.8 copy-start.7
  154.8 1.3 copy-start.2
  156.0 2.2 %copy-start.4 = (f32[24,896]{1,0:T(8,128)S(1)}, f32[24,896]{1,0:T(8,128)}, u32[]{:S(2)}) copy-start(f32[24,896]{1,0:T(8,128)} %copy-done.3) | copy-start | bytes 258052

commit v5 on v4

--- a/solution.py
+++ b/solution.py
@@ -215,22 +215,44 @@
 CHUNKS = 3
 
 
-def grad_kernel(transposed_ref, slope_ref, weight_ref, grad_ref, old_ref):
-    rows = grad_ref.shape[0] // CHUNKS
+def grad_kernel(samples_ref, slope_ref, gram_ref, col_second_ref, grad_ref, new_col_ref, col_root_ref):
+    win, wout = grad_ref.shape
+    rows = win // CHUNKS
+    gram = gram_ref[...]
+    gram_high = gram.astype(bf16)
+    gram_low = (gram - gram_high.astype(f32)).astype(bf16)
+    columns = wout // CHUNKS
+    for i in range(CHUNKS):
+        part = slice(i * columns, (i + 1) * columns)
+        slope = slope_ref[:, part]
+        mixed = jnp.dot(gram_high, slope, preferred_element_type=f32)
+        mixed += jnp.dot(gram_low, slope, preferred_element_type=f32)
+        col_total = jnp.sum(slope.astype(f32) * mixed, axis=0, keepdims=True) * (1.0 / GRAM_SCALE)
+        lines = slice(i * columns // 128, (i + 1) * columns // 128)
+        second = jnp.concatenate([col_second_ref[j : j + 1, :] for j in range(lines.start, lines.stop)], axis=1)
+        new_col = 0.999 * second + 0.001 * (col_total / WIN)
+        new_col_ref[lines, :] = jnp.concatenate([new_col[:, j : j + 128] for j in range(0, columns, 128)], axis=0)
+        col_root_ref[:, part] = jnp.sqrt(new_col)
     for i in range(CHUNKS):
         part = slice(i * rows, (i + 1) * rows)
-        grad_ref[part, :] = jnp.dot(transposed_ref[part, :], slope_ref[...], preferred_element_type=f32)
-        old_ref[part, :] = weight_ref[part, :]
-
-
-def make_grad(transposed, slope, weight):
+        grad_ref[part, :] = lax.dot_general(
+            samples_ref[:, part], slope_ref[...], (((0,), (0,)), ((), ())), preferred_element_type=f32
+        )
+
+
+def make_grad(samples, slope, gram, col_second):
+    shape = (samples.shape[1], slope.shape[1])
     return pl.pallas_call(
         grad_kernel,
-        out_shape=(jax.ShapeDtypeStruct(weight.shape, f32), jax.ShapeDtypeStruct(weight.shape, bf16)),
-        in_specs=[INSIDE] * 3,
-        out_specs=(INSIDE,) * 2,
-        compiler_params=pltpu.CompilerParams(vmem_limit_bytes=20 << 20),
-    )(transposed, slope, weight)
+        out_shape=(
+            jax.ShapeDtypeStruct(shape, f32),
+            jax.ShapeDtypeStruct(col_second.shape, f32),
+            jax.ShapeDtypeStruct((1, shape[1]), f32),
+        ),
+        in_specs=[INSIDE] * 4,
+        out_specs=(INSIDE,) * 3,
+        compiler_params=pltpu.CompilerParams(vmem_limit_bytes=14 << 20),
+    )(samples, slope, gram, col_second)
 
 
 def update_kernel(keep_ref, received_ref, grad_ref, old_ref, row_second_ref, seconds_ref, col_root_ref,
@@ -282,7 +304,7 @@
             pltpu.VMEM((win, wout), bf16),
             pltpu.SemaphoreType.DMA((CHUNKS,)),
         ],
-        compiler_params=pltpu.CompilerParams(vmem_limit_bytes=20 << 20),
+        compiler_params=pltpu.CompilerParams(vmem_limit_bytes=14 << 20),
     )(keep, received, grad, weight, row_second.reshape(-1, 128), seconds, col_root)
 
 
@@ -313,8 +335,8 @@
         sums = jnp.sum(exchange(blocks, axis).astype(f32), axis=0)
 
     packed = pack(place[None], sums, cotangent, row_second.reshape(-1, 128))
-    for axis, size in (("zl", ZL), ("x", X)):
-        packed = gather(packed, axis, size).reshape(packed.shape[0] * size, packed.shape[1])
+    packed = gather(packed, "zl", ZL).reshape(share * ZL, packed.shape[1])
+    packed = lax.all_gather(packed, "x", axis=0, tiled=True)
     other = lax.ppermute(packed, "core", SWAP)
 
     message, seconds, slope, gram = make_message(core[None], packed, other, gathered, weight)
@@ -323,16 +345,11 @@
     keep, send = decoded(zh[None], message)
     received = lax.ppermute(send.astype(f16), "zh", SWAP).astype(f32)
 
-    gram_high, gram_low = split(gram)
-    mixed = jnp.dot(gram_high, slope, preferred_element_type=f32)
-    mixed += jnp.dot(gram_low.astype(bf16), slope, preferred_element_type=f32)
-    col_total = jnp.sum(slope.astype(f32) * mixed, axis=0) / GRAM_SCALE
-    new_col = 0.999 * col_second + 0.001 * (col_total / WIN)
-    grad, old = make_grad(gathered.T, slope, weight)
+    grad, new_col, col_root = make_grad(gathered, slope, gram, col_second.reshape(-1, 128))
     input_grad, new_row, new_weight = update(
-        keep, received, grad, old, row_second, seconds, jnp.sqrt(new_col)[None]
+        keep, received, grad, weight, row_second, seconds, col_root
     )
-    return (input_grad, new_weight, new_row.reshape(win), new_col)
+    return (input_grad, new_weight, new_row.reshape(win), new_col.reshape(wout))
 
 
 def solution(mesh):

time: 162 us -> 160 us (0.988)
  other arithmetic: 2.75 us -> 0.77 us
  local copies, waits for them, and re-layouts: 2.96 us -> 1.29 us
    all_gather x0 -> x1, blocking collectives: none -> 11 us  [local(): packed = lax.all_gather(packed, 'x', axis=0, tiled=True)]
    all_to_all x6 -> x5, blocking collectives: 101 us -> 90.5 us  [exchange(): return lax.all_to_all(blocks, axis, 0, 0)]
    ppermute x1, starting transfers between devices: 7.17 us -> 8.98 us  [local(): other = lax.ppermute(packed, 'core', SWAP)]
  transfers between devices with their start and end apart: 3 -> 3, of which waited for: 2 -> 3; matrix products, arithmetic and copies ran while one was open for 2% -> 1% of each run, Pallas kernels for 1% -> 2%
where the time goes in v5:
time: 160 us
  blocking collectives  117 us (73%)
  starting transfers between devices  22.9 us (14%)
  Pallas kernels  11.5 us (7%)
  waiting for transfers between devices  3.05 us (2%)
  matrix products  2 us (1%)
    all_to_all x5, blocking collectives, exchange(): return lax.all_to_all(blocks, axis, 0, 0)  90.5 us
    all_gather x1, blocking collectives, local(): near = lax.all_gather(samples, 'zh', axis=0, tiled=True)  16.1 us
    all_gather x1, blocking collectives, local(): packed = lax.all_gather(packed, 'x', axis=0, tiled=True)  11 us
    ppermute x1, starting transfers between devices, local(): other = lax.ppermute(packed, 'core', SWAP)  8.98 us
    ppermute x1, starting transfers between devices, local(): received = lax.ppermute(send.astype(f16), 'zh', SWAP).astype(f32)  8.08 us
    ppermute x1, starting transfers between devices, local(): lax.ppermute(partial(theirs).astype(f16), 'core', SWAP).astype(f32)  5.84 us
    pallas_call x1, Pallas kernels, make_message(): pl.pallas_call(message_kernel, out_shape=(jax.ShapeDtypeStruct((COLS, bat...  4.74 us
    pallas_call x1, Pallas kernels, update(): pl.pallas_call(update_kernel, out_shape=(jax.ShapeDtypeStruct((keep.shape...  3.64 us
  transfers between devices with their start and end apart: 3, of which 3 were waited for; matrix products, arithmetic and copies ran while one was open for 1% of the time, Pallas kernels for 2%

profile of v5, /device:TPU:1, one launch (start us, length us, event | category | flops | bytes accessed | tf_op | source)
XLA Modules:
  0.0 159.8 jit_solution(8191483741408910309)
XLA Ops:
  0.6 16.1 %all_gather.6 = bf16[48,768]{1,0:T(8,128)(2,1)S(1)} all-gather(bf16[24,768]{1,0:T(8,128)(2,1)} %param.5), channel_id=1, replica_groups=mesh['x'=4,'zl'=6,'core'=2,'y'=8,'zh'=2] {'zh'}, dimensions={0}, use_global_device_ids=true | all-gather | bytes 110592 | tf_op jit(solution)/shard_map/all_gather | solution.py:322
  16.8 22.5 %all_to_all.25 = bf16[8,48,768]{2,1,0:T(8,128)(2,1)S(1)} all-to-all(bf16[8,48,768]{2,1,0:T(8,128)(2,1)S(1)} %broadcast_in_dim.24), channel_id=1, replica_groups=mesh['x'=4,'zl'=6,'core'=2,'y'=8,'zh'=2] {'y'}, dimensions={0} | all-to-all | bytes 1179648 | tf_op jit(solution)/shard_map/all_to_all | solution.py:27
  39.3 0.0 copy-start
  39.4 0.4 fusion.1
  39.8 1.2 copy-done
  41.0 0.6 convolution_convert_fusion
  41.6 0.2 pad_maximum_fusion
  41.8 5.8 %collective-permute-start = (f16[192,1920]{1,0:T(8,128)(2,1)S(1)}, f16[192,1920]{1,0:T(8,128)(2,1)S(1)}, u32[]{:S(2)}, u32[]{:S(2)}) collective-permute-start(f16[192,1920]{1,0:T(8,128)(2,1)S(1)} %pad_maximum_fusion), channel_id=1, source_target_pairs={{0,16},{16,0},{1,17},{17,1},{2,18},{18,2},{3,19},{19,3},{4,20},{20... | collective-permute-start | bytes 2211848 | tf_op jit(solution)/shard_map/ppermute | solution.py:332
  47.6 0.4 convolution_multiply_fusion
  48.0 0.6 fusion.2
  48.7 0.8 collective-permute-done
  49.5 0.2 fusion
  49.7 15.0 %all_to_all.26 = f16[4,48,1920]{2,1,0:T(8,128)(2,1)S(1)} all-to-all(f16[4,48,1920]{2,1,0:T(8,128)(2,1)S(1)} %bitcast.37), channel_id=1, replica_groups=mesh['x'=4,'zl'=6,'core'=2,'y'=8,'zh'=2] {'x'}, dimensions={0} | all-to-all | bytes 1474560 | tf_op jit(solution)/shard_map/all_to_all | solution.py:27
  64.7 0.1 convert_reduce_fusion
  64.8 16.9 %all_to_all.27 = f16[6,8,1920]{2,1,0:T(8,128)(2,1)S(1)} all-to-all(f16[6,8,1920]{2,1,0:T(8,128)(2,1)S(1)} %convert_bitcast_fusion), channel_id=1, replica_groups=mesh['x'=4,'zl'=6,'core'=2,'y'=8,'zh'=2] {'zl'}, dimensions={0} | all-to-all | bytes 368640 | tf_op jit(solution)/shard_map/all_to_all | solution.py:27
  81.7 0.0 copy-done.1
  81.7 0.0 copy-done.2
  81.7 0.2 shard_map.84
  81.9 12.2 %all_to_all.28 = bf16[6,8,2048]{2,1,0:T(8,128)(2,1)S(1)} all-to-all(bf16[6,8,2048]{2,1,0:T(8,128)(2,1)S(1)} %broadcast_in_dim.25), channel_id=1, replica_groups=mesh['x'=4,'zl'=6,'core'=2,'y'=8,'zh'=2] {'zl'}, dimensions={0} | all-to-all | bytes 393216 | tf_op jit(solution)/shard_map/all_to_all | solution.py:27
  94.1 11.0 %all_gather.7.mine_ref = bf16[192,2048]{1,0:T(8,128)(2,1)S(1)} all-gather(bf16[48,2048]{1,0:T(8,128)(2,1)S(1)} %bitcast.41), channel_id=1, replica_groups=mesh['x'=4,'zl'=6,'core'=2,'y'=8,'zh'=2] {'x'}, dimensions={0}, use_global_device_ids=true | all-gather | bytes 983040 | tf_op jit(solution)/shard_map/all_gather | solution.py:339
  105.1 9.0 %collective-permute-start.1 = (bf16[192,2048]{1,0:T(8,128)(2,1)S(1)}, bf16[192,2048]{1,0:T(8,128)(2,1)S(1)}, u32[]{:S(2)}, u32[]{:S(2)}) collective-permute-start(bf16[192,2048]{1,0:T(8,128)(2,1)S(1)} %all_gather.7.mine_ref), channel_id=1, source_target_pairs={{0,16},{16,0},{1,17},{17,1},{2,18},{18,2},{3,19},{19,3},{4,20},{20... | collective-permute-start | bytes 2359304 | tf_op jit(solution)/shard_map/ppermute | solution.py:340
  114.0 1.9 %collective-permute-done.1.other_ref = bf16[192,2048]{1,0:T(8,128)(2,1)S(1)} collective-permute-done((bf16[192,2048]{1,0:T(8,128)(2,1)S(1)}, bf16[192,2048]{1,0:T(8,128)(2,1)S(1)}, u32[]{:S(2)}, u32[]{:S(2)}) %collective-permute-start.1) | collective-permute-done | bytes 786464 | tf_op jit(solution)/shard_map/ppermute | solution.py:340
  115.9 4.7 %shard_map.85 = (f32[16,24,896]{2,1,0:T(8,128)S(1)}, f32[1,1]{1,0:T(1,128)}, bf16[384,1536]{1,0:T(8,128)(2,1)S(1)}, f32[384,384]{1,0:T(8,128)S(1)}) custom-call(s32[1]{0:T(128)} %bitcast.1.core_ref, bf16[192,2048]{1,0:T(8,128)(2,1)S(1)} %all_gather.7.mine_ref, bf16[192,2048]{1,0:T(8,128)(2,1)S(1)} %collective-permute-done.1.other_ref, ...), custom_call_target="tpu_custom_call" | custom-call | tf_op jit(solution)/shard_map/pallas_call | solution.py:160
  120.7 0.1 convert_element_type.38
  120.8 23.9 %all_to_all.29 = f16[8,2,24,896]{3,2,1,0:T(8,128)(2,1)S(1)} all-to-all(f16[8,2,24,896]{3,2,1,0:T(8,128)(2,1)S(1)} %bitcast.38), channel_id=1, replica_groups=mesh['x'=4,'zl'=6,'core'=2,'y'=8,'zh'=2] {'y'}, dimensions={0} | all-to-all | bytes 1376256 | tf_op jit(solution)/shard_map/all_to_all | solution.py:27
  144.6 0.1 convert_element_type.39.message_ref
  144.7 0.3 shard_map.86
  145.0 8.1 %collective-permute-start.2 = (f16[24,896]{1,0:T(8,128)(2,1)S(1)}, f16[24,896]{1,0:T(8,128)(2,1)S(1)}, u32[]{:S(2)}, u32[]{:S(2)}) collective-permute-start(f16[24,896]{1,0:T(8,128)(2,1)S(1)} %convert_element_type.40), channel_id=1, source_target_pairs={{0,1},{1,0},{2,3},{3,2},{4,5},{5,4},{6,7},{7,6},{8,9},{9,8},{10,11... | collective-permute-start | bytes 129032 | tf_op jit(solution)/shard_map/ppermute | solution.py:346
  153.1 0.0 copy-done.3
  153.1 2.6 %shard_map.87 = (f32[768,1536]{1,0:T(8,128)S(1)}, f32[12,128]{1,0:T(8,128)}, f32[1,1536]{1,0:T(1,128)S(1)}) custom-call(bf16[384,768]{1,0:T(8,128)(2,1)S(1)} %bitcast.29, bf16[384,1536]{1,0:T(8,128)(2,1)S(1)} %get-tuple-element.37.slope_ref, f32[384,384]{1,0:T(8,128)S(1)} %get-tuple-element.38.gram_ref, f32[12,128]{1,0:T(8,128)S(1)} %bitcast.32), custom_call_target="tpu_custom_call" | custom-call | tf_op jit(solution)/shard_map/pallas_call | solution.py:245
  155.8 0.4 collective-permute-done.2
  156.1 3.6 %shard_map.88 = (bf16[24,768]{1,0:T(8,128)(2,1)}, f32[6,128]{1,0:T(8,128)}, bf16[768,1536]{1,0:T(8,128)(2,1)}) custom-call(f32[24,896]{1,0:T(8,128)S(1)} %get-tuple-element.34.keep_ref, f32[24,896]{1,0:T(8,128)S(1)} %convert_element_type.41.received_ref, f32[768,1536]{1,0:T(8,128)S(1)} %get-tuple-element.39.grad_ref, bf16[768,1536]{1,0:T(8,128)(2,1)S(1)} %copy-done, ...), custom_call_target="tpu_custom_call" | custom-call | tf_op jit(solution)/shard_map/pallas_call | solution.py:293
  (11 shorter events, 0.2 us)
Async XLA Ops:
  39.3 1.7 %copy-start = (bf16[768,1536]{1,0:T(8,128)(2,1)S(1)}, bf16[768,1536]{1,0:T(8,128)(2,1)}, u32[]{:S(2)}) copy-start(bf16[768,1536]{1,0:T(8,128)(2,1)} %old_ref.1) | copy-start | bytes 7077892
  41.8 7.7 %collective-permute-start = (f16[192,1920]{1,0:T(8,128)(2,1)S(1)}, f16[192,1920]{1,0:T(8,128)(2,1)S(1)}, u32[]{:S(2)}, u32[]{:S(2)}) collective-permute-start(f16[192,1920]{1,0:T(8,128)(2,1)S(1)} %pad_maximum_fusion), channel_id=1, source_target_pairs={{0,16},{16,0},{1,17},{17,1},{2,18},{18,2},{3,19},{19,3},{4,20},{20... | collective-permute-start | bytes 2211848 | tf_op jit(solution)/shard_map/ppermute | solution.py:332
  64.7 17.0 %copy-start.1 = (bf16[8,1536]{1,0:T(8,128)(2,1)S(1)}, bf16[8,1536]{1,0:T(8,128)(2,1)}, u32[]{:S(2)}) copy-start(bf16[8,1536]{1,0:T(8,128)(2,1)} %cotangent_ref.1) | copy-start | bytes 73732
  64.7 17.0 %copy-start.2 = (f32[768]{0:T(1024)S(1)}, f32[768]{0:T(1024)}, u32[]{:S(2)}) copy-start(f32[768]{0:T(1024)} %param.8) | copy-start | bytes 9220
  105.1 10.9 %collective-permute-start.1 = (bf16[192,2048]{1,0:T(8,128)(2,1)S(1)}, bf16[192,2048]{1,0:T(8,128)(2,1)S(1)}, u32[]{:S(2)}, u32[]{:S(2)}) collective-permute-start(bf16[192,2048]{1,0:T(8,128)(2,1)S(1)} %all_gather.7.mine_ref), channel_id=1, source_target_pairs={{0,16},{16,0},{1,17},{17,1},{2,18},{18,2},{3,19},{19,3},{4,20},{20... | collective-permute-start | bytes 2359304 | tf_op jit(solution)/shard_map/ppermute | solution.py:340
  144.6 8.5 %copy-start.3 = (f32[1536]{0:T(1024)S(1)}, f32[1536]{0:T(1024)}, u32[]{:S(2)}) copy-start(f32[1536]{0:T(1024)} %param.9) | copy-start | bytes 18436
  145.0 11.1 %collective-permute-start.2 = (f16[24,896]{1,0:T(8,128)(2,1)S(1)}, f16[24,896]{1,0:T(8,128)(2,1)S(1)}, u32[]{:S(2)}, u32[]{:S(2)}) collective-permute-start(f16[24,896]{1,0:T(8,128)(2,1)S(1)} %convert_element_type.40), channel_id=1, source_target_pairs={{0,1},{1,0},{2,3},{3,2},{4,5},{5,4},{6,7},{7,6},{8,9},{9,8},{10,11... | collective-permute-start | bytes 129032 | tf_op jit(solution)/shard_map/ppermute | solution.py:346

commit v6 on v5

--- a/solution.py
+++ b/solution.py
@@ -1,3 +1,5 @@
+import functools
+
 import jax
 import jax.numpy as jnp
 from jax import lax
@@ -44,7 +46,10 @@
     return jnp.sum(jnp.sum(value, axis=0, keepdims=True), axis=1, keepdims=True)
 
 
-def encode(own, grad_exp, rows, total):
+SIDE = 16
+
+
+def encode(grad_exp, rows, total):
     row_exp = exponent(jnp.max(jnp.max(rows, axis=0, keepdims=True), axis=1, keepdims=True))
     total_exp = exponent(total)
     rows = rows * jnp.exp2(-row_exp)
@@ -55,7 +60,7 @@
     scalars = jnp.zeros((1, 128), f32)
     for i, value in enumerate((grad_exp, row_exp, total_exp, total_high, (total - total_high) * 256.0)):
         scalars = jnp.where(lanes == i, value, scalars)
-    pad = jnp.zeros((own - 2 * rows.shape[0] - 1, 128), f32)
+    pad = jnp.zeros((SIDE - 2 * rows.shape[0] - 1, 128), f32)
     return jnp.concatenate([rows_high, (rows - rows_high) * 256.0, scalars, pad], axis=0)
 
 
@@ -139,7 +144,7 @@
     top = jnp.max(jnp.max(jnp.abs(slope), axis=0, keepdims=True).astype(f32), axis=1, keepdims=True)
     grad_exp = exponent(top * (WEIGHT_MAX * wout))
     rows = jnp.concatenate([row_total[:, 128 * i : 128 * (i + 1)] for i in range(win // 128)], axis=0)
-    side = encode(own, grad_exp, rows, total)
+    side = encode(grad_exp, rows, total)
     factor = jnp.exp2(-grad_exp)
     each = own // share
     for dest in range(COLS):
@@ -147,8 +152,12 @@
         for block in range(dest * each, (dest + 1) * each):
             start = ((block % CORE) * (ROWS // CORE) + block // CORE) * share
             blocks.append(partial_ref[start : start + share, :])
-        message_ref[dest, :, :win] = jnp.concatenate(blocks, axis=0) * factor
-        message_ref[dest, :, win:] = side
+        grads = jnp.concatenate(blocks, axis=0) * factor
+        for i in range(win // 128):
+            start = (dest % ZH * (win // 128) + i) * own
+            message_ref[dest // ZH, start : start + own, :] = grads[:, 128 * i : 128 * (i + 1)]
+    for y in range(Y):
+        message_ref[y, message_ref.shape[1] - SIDE :, :] = side
 
 
 INSIDE, OUTSIDE = pl.BlockSpec(memory_space=pltpu.VMEM), pl.BlockSpec(memory_space=pltpu.HBM)
@@ -160,7 +169,7 @@
     return pl.pallas_call(
         message_kernel,
         out_shape=(
-            jax.ShapeDtypeStruct((COLS, batch // COLS, win + 128), f32),
+            jax.ShapeDtypeStruct((Y, ZH * (batch // COLS) * (win // 128) + SIDE, 128), f32),
             jax.ShapeDtypeStruct((1, 1), f32),
             jax.ShapeDtypeStruct((batch, weight.shape[1]), bf16),
             jax.ShapeDtypeStruct((batch, batch), f32),
@@ -172,40 +181,40 @@
     )(core, mine, other, samples, weight)
 
 
-def decode(pieces):
-    own, width = pieces[0].shape
-    win = width - 128
-    groups = win // 128
-    scalars = jnp.concatenate([piece[2 * groups : 2 * groups + 1, win:] for piece in pieces], axis=0)
+def decode(sides, groups):
+    scalars = jnp.concatenate([side[2 * groups : 2 * groups + 1, :] for side in sides], axis=0)
     powers = jnp.exp2(scalars)
-    grads = jnp.zeros((own, win), f32)
     sums = jnp.zeros((groups, 128), f32)
-    for i, piece in enumerate(pieces):
-        grads += piece[:, :win] * powers[i : i + 1, 0:1]
-        side = piece[: 2 * groups, win:]
-        sums += (side[:groups] + side[groups:] * (1.0 / 256.0)) * powers[i : i + 1, 1:2]
+    for i, side in enumerate(sides):
+        sums += (side[:groups] + side[groups : 2 * groups] * (1.0 / 256.0)) * powers[i : i + 1, 1:2]
     total = whole((scalars[:, 3:4] + scalars[:, 4:5] * (1.0 / 256.0)) * powers[:, 2:3])
-    return grads, sums, total, jnp.max(scalars[:, 0:1], axis=0, keepdims=True)
-
-
-def decode_kernel(zh_ref, message_ref, keep_ref, send_ref):
+    factors = [powers[i : i + 1, 0:1] for i in range(len(sides))]
+    return factors, sums, total, jnp.max(scalars[:, 0:1], axis=0, keepdims=True)
+
+
+def decode_kernel(groups, zh_ref, message_ref, keep_ref, send_ref):
     zh = zh_ref[0]
-    grads, sums, total, _ = decode([message_ref[i, zh] for i in range(Y)])
-    own, win = grads.shape
-    keep_ref[:, :win] = grads
+    size = keep_ref.shape[0] - SIDE
+    factors, sums, total, grad_exp = decode([message_ref[i, ZH * size :, :] for i in range(Y)], groups)
+
+    def grads(half):
+        rows = pl.ds(pl.multiple_of(half * size, 8), size)
+        return sum(message_ref[i, rows, :] * factors[i] for i in range(Y))
+
     lanes = lax.broadcasted_iota(jnp.int32, (1, 128), 1)
-    rows = [sums, jnp.where(lanes == 0, total, 0.0), jnp.zeros((own - sums.shape[0] - 1, 128), f32)]
-    keep_ref[:, win:] = jnp.concatenate(rows, axis=0)
-    grads, sums, total, grad_exp = decode([message_ref[i, 1 - zh] for i in range(Y)])
+    rows = [sums, jnp.where(lanes == 0, total, 0.0), jnp.zeros((SIDE - groups - 1, 128), f32)]
+    keep_ref[:size, :] = grads(zh)
+    keep_ref[size:, :] = jnp.concatenate(rows, axis=0)
     grad_exp += 3.0
-    send_ref[:, :win] = grads * jnp.exp2(-grad_exp)
-    send_ref[:, win:] = encode(own, grad_exp, sums, total)
-
-
-def decoded(zh, message):
-    return pl.pallas_call(
-        decode_kernel,
-        out_shape=(jax.ShapeDtypeStruct(message.shape[2:], f32),) * 2,
+    send_ref[:size, :] = grads(1 - zh) * jnp.exp2(-grad_exp)
+    send_ref[size:, :] = encode(grad_exp, sums, total)
+
+
+def decoded(zh, message, groups):
+    size = (message.shape[1] - SIDE) // ZH + SIDE
+    return pl.pallas_call(
+        functools.partial(decode_kernel, groups),
+        out_shape=(jax.ShapeDtypeStruct((size, 128), f32),) * 2,
         in_specs=[SCALAR, INSIDE],
         out_specs=(INSIDE,) * 2,
         compiler_params=pltpu.CompilerParams(vmem_limit_bytes=12 << 20),
@@ -265,10 +274,15 @@
         part = pl.ds(i * rows, rows)
         return pltpu.make_async_copy(new_ref.at[part], new_weight_ref.at[part], sems.at[i])
 
-    grads, sums, total, _ = decode([received_ref[...]])
-    input_grad_ref[...] = (grads + keep_ref[:, :win]).astype(bf16)
-    sums += keep_ref[:groups, win:]
-    total += keep_ref[groups : groups + 1, win : win + 1]
+    own = input_grad_ref.shape[0]
+    size = own * groups
+    factors, sums, total, _ = decode([received_ref[size:, :]], groups)
+    for i in range(groups):
+        part = slice(i * own, (i + 1) * own)
+        grads = received_ref[part, :] * factors[0] + keep_ref[part, :]
+        input_grad_ref[:, 128 * i : 128 * (i + 1)] = grads.astype(bf16)
+    sums += keep_ref[size : size + groups, :]
+    total += keep_ref[size + groups : size + groups + 1, :1]
     new_row = 0.999 * row_second_ref[...] + 0.001 * (sums / WOUT)
     new_row_ref[...] = new_row
     scale = 0.999 * (seconds_ref[...] / WIN) + 0.001 * (total / WOUT / WIN)
@@ -288,12 +302,12 @@
         store(i).wait()
 
 
-def update(keep, received, grad, weight, row_second, seconds, col_root):
+def update(own, keep, received, grad, weight, row_second, seconds, col_root):
     win, wout = weight.shape
     return pl.pallas_call(
         update_kernel,
         out_shape=(
-            jax.ShapeDtypeStruct((keep.shape[0], win), bf16),
+            jax.ShapeDtypeStruct((own, win), bf16),
             jax.ShapeDtypeStruct((win // 128, 128), f32),
             jax.ShapeDtypeStruct((win, wout), bf16),
         ),
@@ -335,19 +349,19 @@
         sums = jnp.sum(exchange(blocks, axis).astype(f32), axis=0)
 
     packed = pack(place[None], sums, cotangent, row_second.reshape(-1, 128))
-    packed = gather(packed, "zl", ZL).reshape(share * ZL, packed.shape[1])
-    packed = lax.all_gather(packed, "x", axis=0, tiled=True)
+    for axis, size in (("zl", ZL), ("x", X)):
+        packed = gather(packed, axis, size).reshape(packed.shape[0] * size, packed.shape[1])
     other = lax.ppermute(packed, "core", SWAP)
 
     message, seconds, slope, gram = make_message(core[None], packed, other, gathered, weight)
-    message = exchange(message.astype(f16).reshape(Y, ZH, own, win + 128), "y").astype(f32)
+    message = exchange(message.astype(f16), "y").astype(f32)
     message, slope, gram, gathered = lax.optimization_barrier((message, slope, gram, gathered))
-    keep, send = decoded(zh[None], message)
+    keep, send = decoded(zh[None], message, win // 128)
     received = lax.ppermute(send.astype(f16), "zh", SWAP).astype(f32)
 
     grad, new_col, col_root = make_grad(gathered, slope, gram, col_second.reshape(-1, 128))
     input_grad, new_row, new_weight = update(
-        keep, received, grad, weight, row_second, seconds, col_root
+        own, keep, received, grad, weight, row_second, seconds, col_root
     )
     return (input_grad, new_weight, new_row.reshape(win), new_col.reshape(wout))
 

time: 160 us -> 157 us (0.981)
    all_gather x1 -> x0, blocking collectives: 11 us -> none  [local(): packed = lax.all_gather(packed, 'x', axis=0, tiled=True)]
    all_to_all x5 -> x6, blocking collectives: 90.5 us -> 99.8 us  [exchange(): return lax.all_to_all(blocks, axis, 0, 0)]
    ppermute x1, starting transfers between devices: 8.98 us -> 7.17 us  [local(): other = lax.ppermute(packed, 'core', SWAP)]
  transfers between devices with their start and end apart: 3 -> 3, of which waited for: 3 -> 2; matrix products, arithmetic and copies ran while one was open for 1% -> 1% of each run, Pallas kernels for 2% -> 2%
where the time goes in v6:
time: 157 us; the launch traced here: 156 us
  blocking collectives  116 us (74%)
  starting transfers between devices  21.5 us (14%)
  Pallas kernels  11.4 us (7%)
  waiting for transfers between devices  2.7 us (2%)
  matrix products  2 us (1%)
    all_to_all x6, blocking collectives, exchange(): return lax.all_to_all(blocks, axis, 0, 0)  99.8 us
    all_gather x1, blocking collectives, local(): near = lax.all_gather(samples, 'zh', axis=0, tiled=True)  16.1 us
    ppermute x1, starting transfers between devices, local(): received = lax.ppermute(send.astype(f16), 'zh', SWAP).astype(f32)  8.49 us
    ppermute x1, starting transfers between devices, local(): other = lax.ppermute(packed, 'core', SWAP)  7.17 us
    ppermute x1, starting transfers between devices, local(): lax.ppermute(partial(theirs).astype(f16), 'core', SWAP).astype(f32)  5.84 us
    pallas_call x1, Pallas kernels, make_message(): pl.pallas_call(message_kernel, out_shape=(jax.ShapeDtypeStruct((Y, ZH * (...  4.74 us
    pallas_call x1, Pallas kernels, update(): pl.pallas_call(update_kernel, out_shape=(jax.ShapeDtypeStruct((own, win),...  3.67 us
  transfers between devices with their start and end apart: 3, of which 2 were waited for; matrix products, arithmetic and copies ran while one was open for 1% of the time, Pallas kernels for 2%

profile of v6, /device:TPU:1, one launch (start us, length us, event | category | flops | bytes accessed | tf_op | source)
XLA Modules:
  0.0 156.5 jit_solution(12148086218649863368)
XLA Ops:
  0.6 16.1 %all_gather.3 = bf16[48,768]{1,0:T(8,128)(2,1)S(1)} all-gather(bf16[24,768]{1,0:T(8,128)(2,1)} %param.5), channel_id=1, replica_groups=mesh['x'=4,'zl'=6,'core'=2,'y'=8,'zh'=2] {'zh'}, dimensions={0}, use_global_device_ids=true | all-gather | bytes 110592 | tf_op jit(solution)/shard_map/all_gather | solution.py:336
  16.8 22.5 %all_to_all.30 = bf16[8,48,768]{2,1,0:T(8,128)(2,1)S(1)} all-to-all(bf16[8,48,768]{2,1,0:T(8,128)(2,1)S(1)} %broadcast_in_dim.31), channel_id=1, replica_groups=mesh['x'=4,'zl'=6,'core'=2,'y'=8,'zh'=2] {'y'}, dimensions={0} | all-to-all | bytes 1179648 | tf_op jit(solution)/shard_map/all_to_all | solution.py:29
  39.4 0.4 fusion.1
  39.8 1.2 copy-done
  41.0 0.6 convolution_convert_fusion
  41.6 0.2 pad_maximum_fusion
  41.8 5.8 %collective-permute-start = (f16[192,1920]{1,0:T(8,128)(2,1)S(1)}, f16[192,1920]{1,0:T(8,128)(2,1)S(1)}, u32[]{:S(2)}, u32[]{:S(2)}) collective-permute-start(f16[192,1920]{1,0:T(8,128)(2,1)S(1)} %pad_maximum_fusion), channel_id=1, source_target_pairs={{0,16},{16,0},{1,17},{17,1},{2,18},{18,2},{3,19},{19,3},{4,20},{20... | collective-permute-start | bytes 2211848 | tf_op jit(solution)/shard_map/ppermute | solution.py:346
  47.6 0.4 convolution_multiply_fusion
  48.0 0.6 fusion.2
  48.7 0.8 collective-permute-done
  49.5 0.2 fusion
  49.7 15.0 %all_to_all.31 = f16[4,48,1920]{2,1,0:T(8,128)(2,1)S(1)} all-to-all(f16[4,48,1920]{2,1,0:T(8,128)(2,1)S(1)} %bitcast.39), channel_id=1, replica_groups=mesh['x'=4,'zl'=6,'core'=2,'y'=8,'zh'=2] {'x'}, dimensions={0} | all-to-all | bytes 1474560 | tf_op jit(solution)/shard_map/all_to_all | solution.py:29
  64.7 0.1 convert_reduce_fusion
  64.8 16.9 %all_to_all.32 = f16[6,8,1920]{2,1,0:T(8,128)(2,1)S(1)} all-to-all(f16[6,8,1920]{2,1,0:T(8,128)(2,1)S(1)} %convert_bitcast_fusion), channel_id=1, replica_groups=mesh['x'=4,'zl'=6,'core'=2,'y'=8,'zh'=2] {'zl'}, dimensions={0} | all-to-all | bytes 368640 | tf_op jit(solution)/shard_map/all_to_all | solution.py:29
  81.7 0.0 copy-done.1
  81.7 0.0 copy-done.2
  81.7 0.2 shard_map.84
  81.9 12.2 %all_to_all.33 = bf16[6,8,2048]{2,1,0:T(8,128)(2,1)S(1)} all-to-all(bf16[6,8,2048]{2,1,0:T(8,128)(2,1)S(1)} %broadcast_in_dim.32), channel_id=1, replica_groups=mesh['x'=4,'zl'=6,'core'=2,'y'=8,'zh'=2] {'zl'}, dimensions={0} | all-to-all | bytes 393216 | tf_op jit(solution)/shard_map/all_to_all | solution.py:29
  94.1 0.1 broadcast_in_dim.34
  94.2 10.7 %all_to_all.34 = bf16[4,48,2048]{2,1,0:T(8,128)(2,1)S(1)} all-to-all(bf16[4,48,2048]{2,1,0:T(8,128)(2,1)S(1)} %broadcast_in_dim.34), channel_id=1, replica_groups=mesh['x'=4,'zl'=6,'core'=2,'y'=8,'zh'=2] {'x'}, dimensions={0} | all-to-all | bytes 1572864 | tf_op jit(solution)/shard_map/all_to_all | solution.py:29
  104.9 7.2 %collective-permute-start.1 = (bf16[192,2048]{1,0:T(8,128)(2,1)S(1)}, bf16[192,2048]{1,0:T(8,128)(2,1)S(1)}, u32[]{:S(2)}, u32[]{:S(2)}) collective-permute-start(bf16[192,2048]{1,0:T(8,128)(2,1)S(1)} %bitcast.30), channel_id=1, source_target_pairs={{0,16},{16,0},{1,17},{17,1},{2,18},{18,2},{3,19},{19,3},{4,20},{20... | collective-permute-start | bytes 2359304 | tf_op jit(solution)/shard_map/ppermute | solution.py:354
  112.1 1.9 %collective-permute-done.1.other_ref = bf16[192,2048]{1,0:T(8,128)(2,1)S(1)} collective-permute-done((bf16[192,2048]{1,0:T(8,128)(2,1)S(1)}, bf16[192,2048]{1,0:T(8,128)(2,1)S(1)}, u32[]{:S(2)}, u32[]{:S(2)}) %collective-permute-start.1) | collective-permute-done | bytes 786464 | tf_op jit(solution)/shard_map/ppermute | solution.py:354
  114.0 4.7 %shard_map.85 = (f32[8,304,128]{2,1,0:T(8,128)S(1)}, f32[1,1]{1,0:T(1,128)}, bf16[384,1536]{1,0:T(8,128)(2,1)S(1)}, f32[384,384]{1,0:T(8,128)S(1)}) custom-call(s32[1]{0:T(128)} %bitcast.1.core_ref, bf16[192,2048]{1,0:T(8,128)(2,1)S(1)} %bitcast.31, bf16[192,2048]{1,0:T(8,128)(2,1)S(1)} %collective-permute-done.1.other_ref, bf16[384,768]{1,0:T(8,128)(2,1)S(1)} %bitcast.28, ...), custom_call_target="tpu_custom_call" | custom-call | tf_op jit(solution)/shard_map/pallas_call | solution.py:169
  118.7 0.1 convert_element_type.38
  118.8 22.5 %all_to_all.35 = f16[8,304,128]{2,1,0:T(8,128)(2,1)S(1)} all-to-all(f16[8,304,128]{2,1,0:T(8,128)(2,1)S(1)} %convert_element_type.38), channel_id=1, replica_groups=mesh['x'=4,'zl'=6,'core'=2,'y'=8,'zh'=2] {'y'}, dimensions={0} | all-to-all | bytes 1245184 | tf_op jit(solution)/shard_map/all_to_all | solution.py:29
  141.3 0.1 convert_element_type.39.message_ref
  141.4 0.2 shard_map.86
  141.6 8.5 %collective-permute-start.2 = (f16[160,128]{1,0:T(8,128)(2,1)S(1)}, f16[160,128]{1,0:T(8,128)(2,1)S(1)}, u32[]{:S(2)}, u32[]{:S(2)}) collective-permute-start(f16[160,128]{1,0:T(8,128)(2,1)S(1)} %convert_element_type.40), channel_id=1, source_target_pairs={{0,1},{1,0},{2,3},{3,2},{4,5},{5,4},{6,7},{7,6},{8,9},{9,8},{10,11... | collective-permute-start | bytes 122888 | tf_op jit(solution)/shard_map/ppermute | solution.py:360
  150.1 0.0 copy-done.3
  150.2 2.6 %shard_map.87 = (f32[768,1536]{1,0:T(8,128)S(1)}, f32[12,128]{1,0:T(8,128)}, f32[1,1536]{1,0:T(1,128)S(1)}) custom-call(bf16[384,768]{1,0:T(8,128)(2,1)S(1)} %bitcast.29, bf16[384,1536]{1,0:T(8,128)(2,1)S(1)} %get-tuple-element.37.slope_ref, f32[384,384]{1,0:T(8,128)S(1)} %get-tuple-element.38.gram_ref, f32[12,128]{1,0:T(8,128)S(1)} %bitcast.34), custom_call_target="tpu_custom_call" | custom-call | tf_op jit(solution)/shard_map/pallas_call | solution.py:254
  152.8 0.0 collective-permute-done.2
  152.8 3.7 %shard_map.88 = (bf16[24,768]{1,0:T(8,128)(2,1)}, f32[6,128]{1,0:T(8,128)}, bf16[768,1536]{1,0:T(8,128)(2,1)}) custom-call(f32[160,128]{1,0:T(8,128)S(1)} %get-tuple-element.34.keep_ref, f32[160,128]{1,0:T(8,128)S(1)} %convert_element_type.41.received_ref, f32[768,1536]{1,0:T(8,128)S(1)} %get-tuple-element.39.grad_ref, bf16[768,1536]{1,0:T(8,128)(2,1)S(1)} %copy-done, ...), custom_call_target="tpu_custom_call" | custom-call | tf_op jit(solution)/shard_map/pallas_call | solution.py:307
  (12 shorter events, 0.2 us)
Async XLA Ops:
  39.3 1.7 %copy-start = (bf16[768,1536]{1,0:T(8,128)(2,1)S(1)}, bf16[768,1536]{1,0:T(8,128)(2,1)}, u32[]{:S(2)}) copy-start(bf16[768,1536]{1,0:T(8,128)(2,1)} %old_ref.1) | copy-start | bytes 7077892
  41.8 7.7 %collective-permute-start = (f16[192,1920]{1,0:T(8,128)(2,1)S(1)}, f16[192,1920]{1,0:T(8,128)(2,1)S(1)}, u32[]{:S(2)}, u32[]{:S(2)}) collective-permute-start(f16[192,1920]{1,0:T(8,128)(2,1)S(1)} %pad_maximum_fusion), channel_id=1, source_target_pairs={{0,16},{16,0},{1,17},{17,1},{2,18},{18,2},{3,19},{19,3},{4,20},{20... | collective-permute-start | bytes 2211848 | tf_op jit(solution)/shard_map/ppermute | solution.py:346
  64.7 17.0 %copy-start.1 = (bf16[8,1536]{1,0:T(8,128)(2,1)S(1)}, bf16[8,1536]{1,0:T(8,128)(2,1)}, u32[]{:S(2)}) copy-start(bf16[8,1536]{1,0:T(8,128)(2,1)} %cotangent_ref.1) | copy-start | bytes 73732
  64.7 17.0 %copy-start.2 = (f32[768]{0:T(1024)S(1)}, f32[768]{0:T(1024)}, u32[]{:S(2)}) copy-start(f32[768]{0:T(1024)} %param.8) | copy-start | bytes 9220
  104.9 9.1 %collective-permute-start.1 = (bf16[192,2048]{1,0:T(8,128)(2,1)S(1)}, bf16[192,2048]{1,0:T(8,128)(2,1)S(1)}, u32[]{:S(2)}, u32[]{:S(2)}) collective-permute-start(bf16[192,2048]{1,0:T(8,128)(2,1)S(1)} %bitcast.30), channel_id=1, source_target_pairs={{0,16},{16,0},{1,17},{17,1},{2,18},{18,2},{3,19},{19,3},{4,20},{20... | collective-permute-start | bytes 2359304 | tf_op jit(solution)/shard_map/ppermute | solution.py:354
  141.3 8.8 %copy-start.3 = (f32[1536]{0:T(1024)S(1)}, f32[1536]{0:T(1024)}, u32[]{:S(2)}) copy-start(f32[1536]{0:T(1024)} %param.9) | copy-start | bytes 18436
  141.6 11.1 %collective-permute-start.2 = (f16[160,128]{1,0:T(8,128)(2,1)S(1)}, f16[160,128]{1,0:T(8,128)(2,1)S(1)}, u32[]{:S(2)}, u32[]{:S(2)}) collective-permute-start(f16[160,128]{1,0:T(8,128)(2,1)S(1)} %convert_element_type.40), channel_id=1, source_target_pairs={{0,1},{1,0},{2,3},{3,2},{4,5},{5,4},{6,7},{7,6},{8,9},{9,8},{10,11... | collective-permute-start | bytes 122888 | tf_op jit(solution)/shard_map/ppermute | solution.py:360

commit v7 on v6

--- a/solution.py
+++ b/solution.py
@@ -104,7 +104,24 @@
     )(place, sums, cotangent, row_second)
 
 
-def message_kernel(core_ref, mine_ref, other_ref, samples_ref, weight_ref,
+def early_kernel(mine_ref, weight_ref, early_ref):
+    slope = mine_ref[:, : weight_ref.shape[1]]
+    early_ref[...] = lax.dot_general(slope, weight_ref[...], NT, preferred_element_type=f32)
+
+
+def make_early(mine, weight):
+    rows, (win, wout) = mine.shape[0], weight.shape
+    return pl.pallas_call(
+        early_kernel,
+        out_shape=jax.ShapeDtypeStruct((rows, win), f32),
+        in_specs=[INSIDE] * 2,
+        out_specs=INSIDE,
+        compiler_params=pltpu.CompilerParams(vmem_limit_bytes=14 << 20),
+        cost_estimate=pl.CostEstimate(flops=2 * rows * win * wout, bytes_accessed=2 * win * wout, transcendentals=0),
+    )(mine, weight)
+
+
+def message_kernel(core_ref, early_ref, mine_ref, other_ref, samples_ref, weight_ref,
                    message_ref, seconds_ref, slope_ref, gram_ref, partial_ref):
     batch, win = samples_ref.shape
     wout = weight_ref.shape[1]
@@ -119,7 +136,10 @@
         packed_half.append(both[:, wout:].astype(f32))
     packed_half = jnp.concatenate(packed_half, axis=0)
     slope = slope_ref[...]
-    partial_ref[...] = lax.dot_general(slope, weight_ref[...], NT, preferred_element_type=f32)
+    partial_ref[pl.ds(pl.multiple_of(core_ref[0] * half, 8), half), :] = early_ref[...]
+    partial_ref[pl.ds(pl.multiple_of((1 - core_ref[0]) * half, 8), half), :] = lax.dot_general(
+        other_ref[:, :wout], weight_ref[...], NT, preferred_element_type=f32
+    )
     count = halves(batch)
     lanes = lax.broadcasted_iota(jnp.int32, packed_half.shape, 1)
     there = (lanes >= 2 * count) & (lanes < 2 * count + 3)
@@ -131,7 +151,6 @@
         piece = piece + pltpu.roll(piece, piece.shape[1] - count, 1)
         gram_ref[place * share : (place + 1) * share, :] = pltpu.roll(piece[:, :batch] * times, place * share, 1)
     gram = gram_ref[...]
-    partial_ref[...] = lax.dot_general(slope, weight_ref[...], NT, preferred_element_type=f32)
     mixed = lax.dot_general(slope, slope, NT, preferred_element_type=f32)
     total = whole(mixed * gram) * (1.0 / GRAM_SCALE)
     mixed_high = mixed.astype(bf16)
@@ -164,7 +183,7 @@
 SCALAR = pl.BlockSpec(memory_space=pltpu.SMEM)
 
 
-def make_message(core, mine, other, samples, weight):
+def make_message(core, early, mine, other, samples, weight):
     batch, win = samples.shape
     return pl.pallas_call(
         message_kernel,
@@ -174,11 +193,11 @@
             jax.ShapeDtypeStruct((batch, weight.shape[1]), bf16),
             jax.ShapeDtypeStruct((batch, batch), f32),
         ),
-        in_specs=[SCALAR] + [INSIDE] * 4,
+        in_specs=[SCALAR] + [INSIDE] * 5,
         out_specs=(INSIDE,) * 4,
         scratch_shapes=[pltpu.VMEM((batch, win), f32)],
         compiler_params=pltpu.CompilerParams(vmem_limit_bytes=20 << 20),
-    )(core, mine, other, samples, weight)
+    )(core, early, mine, other, samples, weight)
 
 
 def decode(sides, groups):
@@ -352,8 +371,9 @@
     for axis, size in (("zl", ZL), ("x", X)):
         packed = gather(packed, axis, size).reshape(packed.shape[0] * size, packed.shape[1])
     other = lax.ppermute(packed, "core", SWAP)
-
-    message, seconds, slope, gram = make_message(core[None], packed, other, gathered, weight)
+    early = make_early(packed, weight)
+
+    message, seconds, slope, gram = make_message(core[None], early, packed, other, gathered, weight)
     message = exchange(message.astype(f16), "y").astype(f32)
     message, slope, gram, gathered = lax.optimization_barrier((message, slope, gram, gathered))
     keep, send = decoded(zh[None], message, win // 128)

time: 157 us -> 155 us (0.987)
    pallas_call x1, Pallas kernels: 4.74 us -> 3.07 us  [make_message(): pl.pallas_call(message_kernel, out_shape=(jax.ShapeDtypeStruct((Y, ZH * (...]
where the time goes in v7:
time: 155 us
  blocking collectives  116 us (75%)
  starting transfers between devices  21.5 us (14%)
  Pallas kernels  10.7 us (7%)
  matrix products  2 us (1%)
  waiting for transfers between devices  1.79 us (1%)
    all_to_all x6, blocking collectives, exchange(): return lax.all_to_all(blocks, axis, 0, 0)  99.8 us
    all_gather x1, blocking collectives, local(): near = lax.all_gather(samples, 'zh', axis=0, tiled=True)  16.1 us
    ppermute x1, starting transfers between devices, local(): received = lax.ppermute(send.astype(f16), 'zh', SWAP).astype(f32)  8.49 us
    ppermute x1, starting transfers between devices, local(): other = lax.ppermute(packed, 'core', SWAP)  7.17 us
    ppermute x1, starting transfers between devices, local(): lax.ppermute(partial(theirs).astype(f16), 'core', SWAP).astype(f32)  5.84 us
    pallas_call x1, Pallas kernels, update(): pl.pallas_call(update_kernel, out_shape=(jax.ShapeDtypeStruct((own, win),...  3.67 us
  transfers between devices with their start and end apart: 3, of which 2 were waited for; matrix products, arithmetic and copies ran while one was open for 1% of the time, Pallas kernels for 2%

profile of v7, /device:TPU:1, one launch (start us, length us, event | category | flops | bytes accessed | tf_op | source)
XLA Modules:
  0.0 154.8 jit_solution(11261412962790773507)
XLA Ops:
  0.6 16.1 %all_gather.3 = bf16[48,768]{1,0:T(8,128)(2,1)S(1)} all-gather(bf16[24,768]{1,0:T(8,128)(2,1)} %param.5), channel_id=1, replica_groups=mesh['x'=4,'zl'=6,'core'=2,'y'=8,'zh'=2] {'zh'}, dimensions={0}, use_global_device_ids=true | all-gather | bytes 110592 | tf_op jit(solution)/shard_map/all_gather | solution.py:355
  16.8 22.5 %all_to_all.30 = bf16[8,48,768]{2,1,0:T(8,128)(2,1)S(1)} all-to-all(bf16[8,48,768]{2,1,0:T(8,128)(2,1)S(1)} %broadcast_in_dim.31), channel_id=1, replica_groups=mesh['x'=4,'zl'=6,'core'=2,'y'=8,'zh'=2] {'y'}, dimensions={0} | all-to-all | bytes 1179648 | tf_op jit(solution)/shard_map/all_to_all | solution.py:29
  39.4 0.4 fusion.1
  39.8 1.2 copy-done
  41.0 0.6 convolution_convert_fusion
  41.6 0.2 pad_maximum_fusion
  41.8 5.8 %collective-permute-start = (f16[192,1920]{1,0:T(8,128)(2,1)S(1)}, f16[192,1920]{1,0:T(8,128)(2,1)S(1)}, u32[]{:S(2)}, u32[]{:S(2)}) collective-permute-start(f16[192,1920]{1,0:T(8,128)(2,1)S(1)} %pad_maximum_fusion), channel_id=1, source_target_pairs={{0,16},{16,0},{1,17},{17,1},{2,18},{18,2},{3,19},{19,3},{4,20},{20... | collective-permute-start | bytes 2211848 | tf_op jit(solution)/shard_map/ppermute | solution.py:365
  47.6 0.4 convolution_multiply_fusion
  48.0 0.6 fusion.2
  48.6 0.8 collective-permute-done
  49.5 0.2 fusion
  49.6 15.0 %all_to_all.31 = f16[4,48,1920]{2,1,0:T(8,128)(2,1)S(1)} all-to-all(f16[4,48,1920]{2,1,0:T(8,128)(2,1)S(1)} %bitcast.40), channel_id=1, replica_groups=mesh['x'=4,'zl'=6,'core'=2,'y'=8,'zh'=2] {'x'}, dimensions={0} | all-to-all | bytes 1474560 | tf_op jit(solution)/shard_map/all_to_all | solution.py:29
  64.6 0.1 convert_reduce_fusion
  64.8 16.9 %all_to_all.32 = f16[6,8,1920]{2,1,0:T(8,128)(2,1)S(1)} all-to-all(f16[6,8,1920]{2,1,0:T(8,128)(2,1)S(1)} %convert_bitcast_fusion), channel_id=1, replica_groups=mesh['x'=4,'zl'=6,'core'=2,'y'=8,'zh'=2] {'zl'}, dimensions={0} | all-to-all | bytes 368640 | tf_op jit(solution)/shard_map/all_to_all | solution.py:29
  81.6 0.0 copy-done.1
  81.7 0.0 copy-done.2
  81.7 0.2 shard_map.84
  81.9 12.2 %all_to_all.33 = bf16[6,8,2048]{2,1,0:T(8,128)(2,1)S(1)} all-to-all(bf16[6,8,2048]{2,1,0:T(8,128)(2,1)S(1)} %broadcast_in_dim.32), channel_id=1, replica_groups=mesh['x'=4,'zl'=6,'core'=2,'y'=8,'zh'=2] {'zl'}, dimensions={0} | all-to-all | bytes 393216 | tf_op jit(solution)/shard_map/all_to_all | solution.py:29
  94.1 0.1 broadcast_in_dim.34
  94.1 10.7 %all_to_all.34 = bf16[4,48,2048]{2,1,0:T(8,128)(2,1)S(1)} all-to-all(bf16[4,48,2048]{2,1,0:T(8,128)(2,1)S(1)} %broadcast_in_dim.34), channel_id=1, replica_groups=mesh['x'=4,'zl'=6,'core'=2,'y'=8,'zh'=2] {'x'}, dimensions={0} | all-to-all | bytes 1572864 | tf_op jit(solution)/shard_map/all_to_all | solution.py:29
  104.9 7.2 %collective-permute-start.1 = (bf16[192,2048]{1,0:T(8,128)(2,1)S(1)}, bf16[192,2048]{1,0:T(8,128)(2,1)S(1)}, u32[]{:S(2)}, u32[]{:S(2)}) collective-permute-start(bf16[192,2048]{1,0:T(8,128)(2,1)S(1)} %bitcast.30), channel_id=1, source_target_pairs={{0,16},{16,0},{1,17},{17,1},{2,18},{18,2},{3,19},{19,3},{4,20},{20... | collective-permute-start | bytes 2359304 | tf_op jit(solution)/shard_map/ppermute | solution.py:373
  112.1 0.9 shard_map.85.early_ref
  113.0 1.0 collective-permute-done.1.other_ref
  114.0 3.1 %shard_map.86 = (f32[8,304,128]{2,1,0:T(8,128)S(1)}, f32[1,1]{1,0:T(1,128)}, bf16[384,1536]{1,0:T(8,128)(2,1)S(1)}, f32[384,384]{1,0:T(8,128)S(1)}) custom-call(s32[1]{0:T(128)} %bitcast.1.core_ref, f32[192,768]{1,0:T(8,128)S(1)} %shard_map.85.early_ref, bf16[192,2048]{1,0:T(8,128)(2,1)S(1)} %bitcast.32, ...), custom_call_target="tpu_custom_call" | custom-call | tf_op jit(solution)/shard_map/pallas_call | solution.py:188
  117.0 0.1 convert_element_type.38
  117.1 22.5 %all_to_all.35 = f16[8,304,128]{2,1,0:T(8,128)(2,1)S(1)} all-to-all(f16[8,304,128]{2,1,0:T(8,128)(2,1)S(1)} %convert_element_type.38), channel_id=1, replica_groups=mesh['x'=4,'zl'=6,'core'=2,'y'=8,'zh'=2] {'y'}, dimensions={0} | all-to-all | bytes 1245184 | tf_op jit(solution)/shard_map/all_to_all | solution.py:29
  139.6 0.1 convert_element_type.39.message_ref
  139.7 0.2 shard_map.87
  139.9 8.5 %collective-permute-start.2 = (f16[160,128]{1,0:T(8,128)(2,1)S(1)}, f16[160,128]{1,0:T(8,128)(2,1)S(1)}, u32[]{:S(2)}, u32[]{:S(2)}) collective-permute-start(f16[160,128]{1,0:T(8,128)(2,1)S(1)} %convert_element_type.40), channel_id=1, source_target_pairs={{0,1},{1,0},{2,3},{3,2},{4,5},{5,4},{6,7},{7,6},{8,9},{9,8},{10,11... | collective-permute-start | bytes 122888 | tf_op jit(solution)/shard_map/ppermute | solution.py:380
  148.4 2.6 %shard_map.88 = (f32[768,1536]{1,0:T(8,128)S(1)}, f32[12,128]{1,0:T(8,128)}, f32[1,1536]{1,0:T(1,128)S(1)}) custom-call(bf16[384,768]{1,0:T(8,128)(2,1)S(1)} %bitcast.29, bf16[384,1536]{1,0:T(8,128)(2,1)S(1)} %get-tuple-element.37.slope_ref, f32[384,384]{1,0:T(8,128)S(1)} %get-tuple-element.38.gram_ref, f32[12,128]{1,0:T(8,128)S(1)} %bitcast.35), custom_call_target="tpu_custom_call" | custom-call | tf_op jit(solution)/shard_map/pallas_call | solution.py:273
  151.1 0.0 collective-permute-done.2
  151.1 3.7 %shard_map.89 = (bf16[24,768]{1,0:T(8,128)(2,1)}, f32[6,128]{1,0:T(8,128)}, bf16[768,1536]{1,0:T(8,128)(2,1)}) custom-call(f32[160,128]{1,0:T(8,128)S(1)} %get-tuple-element.34.keep_ref, f32[160,128]{1,0:T(8,128)S(1)} %convert_element_type.41.received_ref, f32[768,1536]{1,0:T(8,128)S(1)} %get-tuple-element.39.grad_ref, bf16[768,1536]{1,0:T(8,128)(2,1)S(1)} %copy-done, ...), custom_call_target="tpu_custom_call" | custom-call | tf_op jit(solution)/shard_map/pallas_call | solution.py:326
  (13 shorter events, 0.2 us)
Async XLA Ops:
  39.3 1.7 %copy-start = (bf16[768,1536]{1,0:T(8,128)(2,1)S(1)}, bf16[768,1536]{1,0:T(8,128)(2,1)}, u32[]{:S(2)}) copy-start(bf16[768,1536]{1,0:T(8,128)(2,1)} %old_ref.1) | copy-start | bytes 7077892
  41.8 7.7 %collective-permute-start = (f16[192,1920]{1,0:T(8,128)(2,1)S(1)}, f16[192,1920]{1,0:T(8,128)(2,1)S(1)}, u32[]{:S(2)}, u32[]{:S(2)}) collective-permute-start(f16[192,1920]{1,0:T(8,128)(2,1)S(1)} %pad_maximum_fusion), channel_id=1, source_target_pairs={{0,16},{16,0},{1,17},{17,1},{2,18},{18,2},{3,19},{19,3},{4,20},{20... | collective-permute-start | bytes 2211848 | tf_op jit(solution)/shard_map/ppermute | solution.py:365
  64.6 17.0 %copy-start.1 = (bf16[8,1536]{1,0:T(8,128)(2,1)S(1)}, bf16[8,1536]{1,0:T(8,128)(2,1)}, u32[]{:S(2)}) copy-start(bf16[8,1536]{1,0:T(8,128)(2,1)} %cotangent_ref.1) | copy-start | bytes 73732
  64.6 17.0 %copy-start.2 = (f32[768]{0:T(1024)S(1)}, f32[768]{0:T(1024)}, u32[]{:S(2)}) copy-start(f32[768]{0:T(1024)} %param.8) | copy-start | bytes 9220
  104.9 9.1 %collective-permute-start.1 = (bf16[192,2048]{1,0:T(8,128)(2,1)S(1)}, bf16[192,2048]{1,0:T(8,128)(2,1)S(1)}, u32[]{:S(2)}, u32[]{:S(2)}) collective-permute-start(bf16[192,2048]{1,0:T(8,128)(2,1)S(1)} %bitcast.30), channel_id=1, source_target_pairs={{0,16},{16,0},{1,17},{17,1},{2,18},{18,2},{3,19},{19,3},{4,20},{20... | collective-permute-start | bytes 2359304 | tf_op jit(solution)/shard_map/ppermute | solution.py:373
  139.6 8.8 %copy-start.3 = (f32[1536]{0:T(1024)S(1)}, f32[1536]{0:T(1024)}, u32[]{:S(2)}) copy-start(f32[1536]{0:T(1024)} %param.9) | copy-start | bytes 18436
  139.9 11.1 %collective-permute-start.2 = (f16[160,128]{1,0:T(8,128)(2,1)S(1)}, f16[160,128]{1,0:T(8,128)(2,1)S(1)}, u32[]{:S(2)}, u32[]{:S(2)}) collective-permute-start(f16[160,128]{1,0:T(8,128)(2,1)S(1)} %convert_element_type.40), channel_id=1, source_target_pairs={{0,1},{1,0},{2,3},{3,2},{4,5},{5,4},{6,7},{7,6},{8,9},{9,8},{10,11... | collective-permute-start | bytes 122888 | tf_op jit(solution)/shard_map/ppermute | solution.py:380

commit v8 on v7

--- a/solution.py
+++ b/solution.py
@@ -71,15 +71,37 @@
     return batch // 2 + batch // ROWS
 
 
-def pack_kernel(place_ref, sums_ref, cotangent_ref, row_second_ref, packed_ref):
+def gram_kernel(rows_ref, others_ref, half_ref):
+    width = half_ref.shape[1]
+    share = rows_ref.shape[0] * CORE // ROWS
+    rows = rows_ref[...]
+    gram = [lax.dot_general(rows, side, NT, preferred_element_type=f32) for side in (rows, others_ref[...])]
+    gram = jnp.concatenate(gram, axis=1) * GRAM_SCALE
+    batch = gram.shape[1]
+    for place in range(ROWS // CORE):
+        part = slice(place * share, (place + 1) * share)
+        half_ref[part, :] = pltpu.roll(gram[part, :], (batch - place * share) % batch, 1)[:, :width]
+
+
+def make_gram(rows, others):
+    batch = rows.shape[0] * CORE
+    width = min(batch, -(-halves(batch) // 128) * 128)
+    return pl.pallas_call(
+        gram_kernel,
+        out_shape=jax.ShapeDtypeStruct((rows.shape[0], width), f32),
+        in_specs=[INSIDE] * 2,
+        out_specs=INSIDE,
+        compiler_params=pltpu.CompilerParams(vmem_limit_bytes=14 << 20),
+    )(rows, others)
+
+
+def pack_kernel(sums_ref, cotangent_ref, row_second_ref, packed_ref):
     share, wout = cotangent_ref.shape
-    batch = sums_ref.shape[1] - wout
     side = packed_ref.shape[1] - wout
-    count = halves(batch)
+    count = halves(share * ROWS)
     packed_ref[:, :wout] = (cotangent_ref[...].astype(f32) * silu_slope(sums_ref[:, :wout])).astype(bf16)
-    shift = lax.rem(batch - place_ref[0] * share, batch)
-    gram = pltpu.roll(sums_ref[:, wout:], shift, 1)
-    gram = jnp.concatenate([gram, jnp.zeros((share, side - batch), f32)], axis=1)
+    gram = sums_ref[:, wout:]
+    gram = jnp.concatenate([gram, jnp.zeros((share, side - gram.shape[1]), f32)], axis=1)
     high = gram.astype(bf16).astype(f32)
     low = pltpu.roll(gram - high, count, 1)
     lanes = lax.broadcasted_iota(jnp.int32, (share, side), 1)
@@ -92,16 +114,16 @@
     packed_ref[:, wout:] = out.astype(bf16)
 
 
-def pack(place, sums, cotangent, row_second):
+def pack(sums, cotangent, row_second):
     share, wout = cotangent.shape
-    width = wout + -(-(2 * halves(sums.shape[1] - wout) + 3) // 128) * 128
+    width = wout + -(-(2 * halves(share * ROWS) + 3) // 128) * 128
     return pl.pallas_call(
         pack_kernel,
         out_shape=jax.ShapeDtypeStruct((share, width), bf16),
-        in_specs=[pl.BlockSpec(memory_space=pltpu.SMEM)] + [pl.BlockSpec(memory_space=pltpu.VMEM)] * 3,
-        out_specs=pl.BlockSpec(memory_space=pltpu.VMEM),
+        in_specs=[INSIDE] * 3,
+        out_specs=INSIDE,
         compiler_params=pltpu.CompilerParams(vmem_limit_bytes=16 << 20),
-    )(place, sums, cotangent, row_second)
+    )(sums, cotangent, row_second)
 
 
 def early_kernel(mine_ref, weight_ref, early_ref):
@@ -349,8 +371,7 @@
     share, wout = cotangent.shape
     batch = own * COLS
     core, zh = lax.axis_index("core").astype(jnp.int32), lax.axis_index("zh").astype(jnp.int32)
-    place = ((core * X + lax.axis_index("x")) * ZL + lax.axis_index("zl")).astype(jnp.int32)
-    samples, core, zh, place, first = lax.optimization_barrier((samples, core, zh, place, core == 0))
+    samples, core, zh, first = lax.optimization_barrier((samples, core, zh, core == 0))
 
     near = lax.all_gather(samples, "zh", axis=0, tiled=True)
     gathered = gather(near, "y", Y).reshape(X, ZL, CORE, share, win).transpose(2, 0, 1, 3, 4)
@@ -358,16 +379,16 @@
     theirs = jnp.where(first, gathered[1], gathered[0]).reshape(batch // CORE, win)
     gathered = gathered.reshape(batch, win)
 
-    def partial(rows):
-        gram = lax.dot_general(rows, gathered, NT, preferred_element_type=f32)
-        return jnp.concatenate([jnp.dot(rows, weight, preferred_element_type=f32), gram * GRAM_SCALE], axis=1)
-
-    sums = lax.ppermute(partial(theirs).astype(f16), "core", SWAP).astype(f32) + partial(mine)
+    def partial(rows, others):
+        product = jnp.dot(rows, weight, preferred_element_type=f32)
+        return jnp.concatenate([product, make_gram(rows, others)], axis=1)
+
+    sums = lax.ppermute(partial(theirs, mine).astype(f16), "core", SWAP).astype(f32) + partial(mine, theirs)
     for axis, size in (("x", X), ("zl", ZL)):
         blocks = sums.astype(f16).reshape(size, sums.shape[0] // size, sums.shape[1])
         sums = jnp.sum(exchange(blocks, axis).astype(f32), axis=0)
 
-    packed = pack(place[None], sums, cotangent, row_second.reshape(-1, 128))
+    packed = pack(sums, cotangent, row_second.reshape(-1, 128))
     for axis, size in (("zl", ZL), ("x", X)):
         packed = gather(packed, axis, size).reshape(packed.shape[0] * size, packed.shape[1])
     other = lax.ppermute(packed, "core", SWAP)

time: 155 us -> 153 us (0.987)
  transfers between devices with their start and end apart: 3 -> 3, of which waited for: 2 -> 2; matrix products, arithmetic and copies ran while one was open for 1% -> 0% of each run, Pallas kernels for 2% -> 3%
where the time goes in v8:
time: 153 us
  blocking collectives  115 us (75%)
  starting transfers between devices  21.5 us (14%)
  Pallas kernels  11.5 us (8%)
  waiting for transfers between devices  1.56 us (1%)
    all_to_all x6, blocking collectives, exchange(): return lax.all_to_all(blocks, axis, 0, 0)  99.1 us
    all_gather x1, blocking collectives, local(): near = lax.all_gather(samples, 'zh', axis=0, tiled=True)  16.1 us
    ppermute x1, starting transfers between devices, local(): received = lax.ppermute(send.astype(f16), 'zh', SWAP).astype(f32)  8.55 us
    ppermute x1, starting transfers between devices, local(): other = lax.ppermute(packed, 'core', SWAP)  7.1 us
    ppermute x1, starting transfers between devices, local(): lax.ppermute(partial(theirs, mine).astype(f16), 'core', SWAP).astype(f32)  5.84 us
    pallas_call x1, Pallas kernels, update(): pl.pallas_call(update_kernel, out_shape=(jax.ShapeDtypeStruct((own, win),...  3.63 us
    pallas_call x1, Pallas kernels, make_message(): pl.pallas_call(message_kernel, out_shape=(jax.ShapeDtypeStruct((Y, ZH * (...  3.07 us
  transfers between devices with their start and end apart: 3, of which 2 were waited for; matrix products, arithmetic and copies ran while one was open for 0% of the time, Pallas kernels for 3%

profile of v8, /device:TPU:1, one launch (start us, length us, event | category | flops | bytes accessed | tf_op | source)
XLA Modules:
  0.0 152.7 jit_solution(4965467656293449479)
XLA Ops:
  0.6 16.1 %all_gather.3 = bf16[48,768]{1,0:T(8,128)(2,1)S(1)} all-gather(bf16[24,768]{1,0:T(8,128)(2,1)} %param.5), channel_id=1, replica_groups=mesh['x'=4,'zl'=6,'core'=2,'y'=8,'zh'=2] {'zh'}, dimensions={0}, use_global_device_ids=true | all-gather | bytes 110592 | tf_op jit(solution)/shard_map/all_gather | solution.py:376
  16.8 0.0 copy-start
  16.8 22.7 %all_to_all.30 = bf16[8,48,768]{2,1,0:T(8,128)(2,1)S(1)} all-to-all(bf16[8,48,768]{2,1,0:T(8,128)(2,1)S(1)} %broadcast_in_dim.27), channel_id=1, replica_groups=mesh['x'=4,'zl'=6,'core'=2,'y'=8,'zh'=2] {'y'}, dimensions={0} | all-to-all | bytes 1179648 | tf_op jit(solution)/shard_map/all_to_all | solution.py:29
  39.5 0.5 shard_map.84
  40.0 0.0 copy-done
  40.0 0.6 convolution_convert_fusion
  40.6 0.2 pad_maximum_fusion
  40.8 5.8 %collective-permute-start = (f16[192,1792]{1,0:T(8,128)(2,1)S(1)}, f16[192,1792]{1,0:T(8,128)(2,1)S(1)}, u32[]{:S(2)}, u32[]{:S(2)}) collective-permute-start(f16[192,1792]{1,0:T(8,128)(2,1)S(1)} %pad_maximum_fusion), channel_id=1, source_target_pairs={{0,16},{16,0},{1,17},{17,1},{2,18},{18,2},{3,19},{19,3},{4,20},{20... | collective-permute-start | bytes 2064392 | tf_op jit(solution)/shard_map/ppermute | solution.py:386
  46.7 0.5 shard_map.85
  47.2 0.6 fusion.1
  47.8 0.6 collective-permute-done
  48.4 0.2 fusion
  48.6 14.5 %all_to_all.31 = f16[4,48,1792]{2,1,0:T(8,128)(2,1)S(1)} all-to-all(f16[4,48,1792]{2,1,0:T(8,128)(2,1)S(1)} %bitcast.37), channel_id=1, replica_groups=mesh['x'=4,'zl'=6,'core'=2,'y'=8,'zh'=2] {'x'}, dimensions={0} | all-to-all | bytes 1376256 | tf_op jit(solution)/shard_map/all_to_all | solution.py:29
  63.1 0.1 convert_reduce_fusion
  63.2 16.7 %all_to_all.32 = f16[6,8,1792]{2,1,0:T(8,128)(2,1)S(1)} all-to-all(f16[6,8,1792]{2,1,0:T(8,128)(2,1)S(1)} %convert_bitcast_fusion), channel_id=1, replica_groups=mesh['x'=4,'zl'=6,'core'=2,'y'=8,'zh'=2] {'zl'}, dimensions={0} | all-to-all | bytes 344064 | tf_op jit(solution)/shard_map/all_to_all | solution.py:29
  79.9 0.1 shard_map.86
  80.0 12.1 %all_to_all.33 = bf16[6,8,2048]{2,1,0:T(8,128)(2,1)S(1)} all-to-all(bf16[6,8,2048]{2,1,0:T(8,128)(2,1)S(1)} %broadcast_in_dim.28), channel_id=1, replica_groups=mesh['x'=4,'zl'=6,'core'=2,'y'=8,'zh'=2] {'zl'}, dimensions={0} | all-to-all | bytes 393216 | tf_op jit(solution)/shard_map/all_to_all | solution.py:29
  92.1 0.1 broadcast_in_dim.30
  92.2 10.7 %all_to_all.34 = bf16[4,48,2048]{2,1,0:T(8,128)(2,1)S(1)} all-to-all(bf16[4,48,2048]{2,1,0:T(8,128)(2,1)S(1)} %broadcast_in_dim.30), channel_id=1, replica_groups=mesh['x'=4,'zl'=6,'core'=2,'y'=8,'zh'=2] {'x'}, dimensions={0} | all-to-all | bytes 1572864 | tf_op jit(solution)/shard_map/all_to_all | solution.py:29
  102.9 7.1 %collective-permute-start.1 = (bf16[192,2048]{1,0:T(8,128)(2,1)S(1)}, bf16[192,2048]{1,0:T(8,128)(2,1)S(1)}, u32[]{:S(2)}, u32[]{:S(2)}) collective-permute-start(bf16[192,2048]{1,0:T(8,128)(2,1)S(1)} %bitcast.21), channel_id=1, source_target_pairs={{0,16},{16,0},{1,17},{17,1},{2,18},{18,2},{3,19},{19,3},{4,20},{20... | collective-permute-start | bytes 2359304 | tf_op jit(solution)/shard_map/ppermute | solution.py:394
  110.1 0.9 shard_map.87.early_ref
  111.0 0.9 collective-permute-done.1.other_ref
  111.9 3.1 %shard_map.88 = (f32[8,304,128]{2,1,0:T(8,128)S(1)}, f32[1,1]{1,0:T(1,128)}, bf16[384,1536]{1,0:T(8,128)(2,1)S(1)}, f32[384,384]{1,0:T(8,128)S(1)}) custom-call(s32[1]{0:T(128)} %bitcast.1.core_ref, f32[192,768]{1,0:T(8,128)S(1)} %shard_map.87.early_ref, bf16[192,2048]{1,0:T(8,128)(2,1)S(1)} %bitcast.23, ...), custom_call_target="tpu_custom_call" | custom-call | tf_op jit(solution)/shard_map/pallas_call | solution.py:210
  115.0 0.1 convert_element_type.38
  115.1 22.5 %all_to_all.35 = f16[8,304,128]{2,1,0:T(8,128)(2,1)S(1)} all-to-all(f16[8,304,128]{2,1,0:T(8,128)(2,1)S(1)} %convert_element_type.38), channel_id=1, replica_groups=mesh['x'=4,'zl'=6,'core'=2,'y'=8,'zh'=2] {'y'}, dimensions={0} | all-to-all | bytes 1245184 | tf_op jit(solution)/shard_map/all_to_all | solution.py:29
  137.6 0.1 convert_element_type.39.message_ref
  137.7 0.2 shard_map.89
  137.9 8.5 %collective-permute-start.2 = (f16[160,128]{1,0:T(8,128)(2,1)S(1)}, f16[160,128]{1,0:T(8,128)(2,1)S(1)}, u32[]{:S(2)}, u32[]{:S(2)}) collective-permute-start(f16[160,128]{1,0:T(8,128)(2,1)S(1)} %convert_element_type.40), channel_id=1, source_target_pairs={{0,1},{1,0},{2,3},{3,2},{4,5},{5,4},{6,7},{7,6},{8,9},{9,8},{10,11... | collective-permute-start | bytes 122888 | tf_op jit(solution)/shard_map/ppermute | solution.py:401
  146.5 0.0 copy-done.3
  146.5 2.6 %shard_map.90 = (f32[768,1536]{1,0:T(8,128)S(1)}, f32[12,128]{1,0:T(8,128)}, f32[1,1536]{1,0:T(1,128)S(1)}) custom-call(bf16[384,768]{1,0:T(8,128)(2,1)S(1)} %bitcast.28, bf16[384,1536]{1,0:T(8,128)(2,1)S(1)} %get-tuple-element.35.slope_ref, f32[384,384]{1,0:T(8,128)S(1)} %get-tuple-element.36.gram_ref, f32[12,128]{1,0:T(8,128)S(1)} %bitcast.34), custom_call_target="tpu_custom_call" | custom-call | tf_op jit(solution)/shard_map/pallas_call | solution.py:295
  149.1 0.0 collective-permute-done.2
  149.1 3.6 %shard_map.91 = (bf16[24,768]{1,0:T(8,128)(2,1)}, f32[6,128]{1,0:T(8,128)}, bf16[768,1536]{1,0:T(8,128)(2,1)}) custom-call(f32[160,128]{1,0:T(8,128)S(1)} %get-tuple-element.32.keep_ref, f32[160,128]{1,0:T(8,128)S(1)} %convert_element_type.41.received_ref, f32[768,1536]{1,0:T(8,128)S(1)} %get-tuple-element.37.grad_ref, bf16[768,1536]{1,0:T(8,128)(2,1)S(1)} %copy-done, ...), custom_call_target="tpu_custom_call" | custom-call | tf_op jit(solution)/shard_map/pallas_call | solution.py:348
  (14 shorter events, 0.2 us)
Async XLA Ops:
  16.8 23.3 %copy-start = (bf16[768,1536]{1,0:T(8,128)(2,1)S(1)}, bf16[768,1536]{1,0:T(8,128)(2,1)}, u32[]{:S(2)}) copy-start(bf16[768,1536]{1,0:T(8,128)(2,1)} %old_ref.1) | copy-start | bytes 7077892
  40.8 7.6 %collective-permute-start = (f16[192,1792]{1,0:T(8,128)(2,1)S(1)}, f16[192,1792]{1,0:T(8,128)(2,1)S(1)}, u32[]{:S(2)}, u32[]{:S(2)}) collective-permute-start(f16[192,1792]{1,0:T(8,128)(2,1)S(1)} %pad_maximum_fusion), channel_id=1, source_target_pairs={{0,16},{16,0},{1,17},{17,1},{2,18},{18,2},{3,19},{19,3},{4,20},{20... | collective-permute-start | bytes 2064392 | tf_op jit(solution)/shard_map/ppermute | solution.py:386
  63.1 16.8 %copy-start.1 = (bf16[8,1536]{1,0:T(8,128)(2,1)S(1)}, bf16[8,1536]{1,0:T(8,128)(2,1)}, u32[]{:S(2)}) copy-start(bf16[8,1536]{1,0:T(8,128)(2,1)} %cotangent_ref.1) | copy-start | bytes 73732
  63.1 16.8 %copy-start.2 = (f32[768]{0:T(1024)S(1)}, f32[768]{0:T(1024)}, u32[]{:S(2)}) copy-start(f32[768]{0:T(1024)} %param.8) | copy-start | bytes 9220
  102.9 9.0 %collective-permute-start.1 = (bf16[192,2048]{1,0:T(8,128)(2,1)S(1)}, bf16[192,2048]{1,0:T(8,128)(2,1)S(1)}, u32[]{:S(2)}, u32[]{:S(2)}) collective-permute-start(bf16[192,2048]{1,0:T(8,128)(2,1)S(1)} %bitcast.21), channel_id=1, source_target_pairs={{0,16},{16,0},{1,17},{17,1},{2,18},{18,2},{3,19},{19,3},{4,20},{20... | collective-permute-start | bytes 2359304 | tf_op jit(solution)/shard_map/ppermute | solution.py:394
  137.6 8.9 %copy-start.3 = (f32[1536]{0:T(1024)S(1)}, f32[1536]{0:T(1024)}, u32[]{:S(2)}) copy-start(f32[1536]{0:T(1024)} %param.9) | copy-start | bytes 18436
  137.9 11.2 %collective-permute-start.2 = (f16[160,128]{1,0:T(8,128)(2,1)S(1)}, f16[160,128]{1,0:T(8,128)(2,1)S(1)}, u32[]{:S(2)}, u32[]{:S(2)}) collective-permute-start(f16[160,128]{1,0:T(8,128)(2,1)S(1)} %convert_element_type.40), channel_id=1, source_target_pairs={{0,1},{1,0},{2,3},{3,2},{4,5},{5,4},{6,7},{7,6},{8,9},{9,8},{10,11... | collective-permute-start | bytes 122888 | tf_op jit(solution)/shard_map/ppermute | solution.py:401
